TPU v7x, 32 devices: a whole 2x2x4 slice. The times are simulated.
32 devices in a mesh: groups: 2 (over y), expert: 8 (over z, x), dp: 2 (over core).
Axes of the slice: x: 2, y: 2, z: 4, core: 2. Of those that a mesh axis runs over, the one named last changes fastest.
Arguments:
- queries: bfloat16 [128, 8, 576], P(('groups', 'dp'), 'expert'), parts along dimension 0, may hold values from -400 to 400
- kv_pages: bfloat16 [128, 64, 576], P(('groups', 'dp')), parts along dimension 0, may hold values from -10 to 10
- page_tables: int32 [128, 8], P(('groups', 'dp')), parts along dimension 0, may hold values from 0 to 31, as said below
- lengths: int32 [128], P(('groups', 'dp')), parts along dimension 0, may hold values from 2 to 512
- owners: int32 [128], P(('groups', 'dp')), parts along dimension 0, may hold values from 0 to 7, as said below
- up_values: bfloat16 [8, 512, 128], P('expert'), may hold values from -0.25 to 0.25
- out_proj: bfloat16 [8, 128, 3584], P('expert'), may hold values from -0.1875 to 0.1875
- residual: bfloat16 [128, 3584], P(('groups', 'expert', 'dp')), parts along dimension 0, may hold values from -0.59765625 to 0.59765625
- verify_states: bfloat16 [128, 2, 3584], P(('groups', 'expert', 'dp')), parts along dimension 0, may hold values from -6 to 6
- norm_gain: bfloat16 [3584], replicated, may hold values from 0.099609375 to 1.8984375
- route_ids: int32 [128, 3, 8], P(('groups', 'expert', 'dp')), parts along dimension 0, may hold values from 0 to 15, all different within a row; in each aligned block of 12 rows (0 to 11, 12 to 23, ..., all dimensions but the last counted through in order) at most 12 rows name the same one
- route_weights: float32 [128, 3, 8], P(('groups', 'expert', 'dp')), parts along dimension 0, may hold values from 0.05 to 1
- expert_up: bfloat16 [16, 3584, 1024], P(('expert', 'dp')), may hold values from -0.09375 to 0.09375
Outputs:
- moe_slots: bfloat16 [128, 3, 8, 1024], P(('groups', 'expert', 'dp')), parts along dimension 0
There are 2 independent parts, one for each index of `groups`. A program takes and returns all parts, laid end to end along the dimension named above; an argument that names none is the same for every part. Nothing has to cross between parts.
Inputs may be any that keep to these rules, and one draw needn't show every extreme that they name: `page_tables`: each row names 8 different pages, numbered within its block of 32 rows. `owners`: in each block of 32 rows every owner is named exactly 4 times. `route_ids`: A token's 8 experts differ; in the rows of one device no expert is named more than 12 times.
All inputs are finite; a program needn't handle non-finite values.
Results may differ from a plain program's by a relative error of at most 0.0064.
Values may be sent and summed in bfloat16 or wider, within the bound.
No kernel may reach another device: no remote copies, remote signals or barrier semaphores. Data moves between devices by JAX's collectives and lax.ppermute only.
A program may use at most 64 MiB of HBM per device.

v0:
```python
import jax
import jax.numpy as jnp
from jax import lax
from jax.sharding import PartitionSpec as P

D = 3584
LATENT = 512
ROPE = 64
VHEAD = 128
HE = 1024
TOPK = 8
VERIFY = 3


def block_values(query_block, table_block, length_block, pages, up_head):
    page_total, page_len, key_width = pages.shape
    table_len = table_block.shape[1]
    present = table_block[:, :, None] == jnp.arange(page_total, dtype=jnp.int32)[None, None, :]
    slot_index = jnp.sum(
        jnp.where(present, jnp.arange(table_len, dtype=jnp.int32)[None, :, None], 0), axis=1
    )
    member = jnp.any(present, axis=1)
    positions = (
        slot_index[:, :, None] * page_len + jnp.arange(page_len, dtype=jnp.int32)[None, None, :]
    )
    visible = member[:, :, None] & (positions < length_block[:, None, None])
    visible = visible.reshape(query_block.shape[0], page_total * page_len)
    keys_flat = pages.reshape(page_total * page_len, key_width)
    scores = jnp.dot(query_block, keys_flat.T, preferred_element_type=jnp.float32) * (
        VHEAD + ROPE
    ) ** (-0.5)
    masked = jnp.where(visible, scores, -1e30)
    row_max = jnp.max(masked, axis=1, keepdims=True)
    exponent = jnp.where(visible, jnp.exp(masked - row_max), 0.0)
    attention = (exponent / jnp.sum(exponent, axis=1, keepdims=True)).astype(jnp.bfloat16)
    context = jnp.dot(attention, keys_flat[:, :LATENT], preferred_element_type=jnp.float32).astype(
        jnp.bfloat16
    )
    return jnp.dot(context, up_head, preferred_element_type=jnp.float32).astype(jnp.bfloat16)


def per_device(
    queries,
    kv_pages,
    page_tables,
    lengths,
    owners,
    up_values,
    out_proj,
    residual,
    verify_states,
    norm_gain,
    route_ids,
    route_weights,
    expert_up,
):
    row_count = queries.shape[0]
    verify_rows = residual.shape[0]
    block_size = min(512, row_count)
    block_count = row_count // block_size
    head_idx = 0
    up_head = up_values[head_idx]

    def run_block(inputs):
        query_block, table_block, length_block = inputs
        return block_values(query_block, table_block, length_block, kv_pages, up_head)

    mapped = lax.map(
        run_block,
        (
            queries[:, head_idx, :].reshape(block_count, block_size, -1),
            page_tables.reshape(block_count, block_size, -1),
            lengths.reshape(block_count, block_size),
        ),
    )
    head_values = [mapped.reshape(row_count, -1)]
    row_order = jnp.argsort(owners, stable=True)
    sorted_values = [values[row_order] for values in head_values]
    head_idx = 0
    picked = sorted_values[head_idx]
    summed = jnp.dot(picked, out_proj[head_idx], preferred_element_type=jnp.float32)
    hidden_sum = lax.psum_scatter(summed, "expert", scatter_dimension=0, tiled=True)
    states = jnp.concatenate(
        [
            (residual.astype(jnp.float32) + hidden_sum)[:, None, :],
            verify_states.astype(jnp.float32),
        ],
        axis=1,
    )
    normed = (
        states
        * lax.rsqrt(jnp.mean(states * states, axis=-1, keepdims=True) + 1e-06)
        * norm_gain.astype(jnp.float32)
    )
    token_rows = normed.astype(jnp.bfloat16).reshape(verify_rows * VERIFY, D)
    experts = lax.axis_size("expert") * lax.axis_size("dp")
    capacity = max(
        2, min(VERIFY * verify_rows, (2 * VERIFY * verify_rows * TOPK + experts - 1) // experts)
    )
    route_flat = route_ids.reshape(-1)
    chosen = route_flat[:, None] == jnp.arange(experts, dtype=jnp.int32)[None, :]
    running = jnp.cumsum(chosen.astype(jnp.int32), axis=0) - 1
    slot_rank = jnp.sum(jnp.where(chosen, running, 0), axis=1)
    outgoing = (
        jnp.zeros((experts, capacity, D), jnp.bfloat16)
        .at[route_flat, slot_rank]
        .set(jnp.repeat(token_rows, TOPK, axis=0))
    )
    weight_here = expert_up[0]
    product = jnp.einsum(
        "scd,dh->sch",
        lax.all_to_all(outgoing, ("expert", "dp"), split_axis=0, concat_axis=0, tiled=True),
        weight_here,
        preferred_element_type=jnp.float32,
    )
    returned = lax.all_to_all(
        jax.nn.silu(product).astype(jnp.bfloat16),
        ("expert", "dp"),
        split_axis=0,
        concat_axis=0,
        tiled=True,
    )
    activation = returned[route_flat, slot_rank]
    weighted = route_weights.reshape(-1, 1) * activation.astype(jnp.float32)
    return weighted.astype(jnp.bfloat16).reshape(verify_rows, VERIFY, TOPK, HE)


def solution(mesh):
    placed = (
        P(("groups", "dp"), "expert", None),
        P(("groups", "dp"), None, None),
        P(("groups", "dp"), None),
        P(("groups", "dp")),
        P(("groups", "dp")),
        P("expert", None, None),
        P("expert", None, None),
        P(("groups", "expert", "dp"), None),
        P(("groups", "expert", "dp"), None, None),
        P(),
        P(("groups", "expert", "dp"), None, None),
        P(("groups", "expert", "dp"), None, None),
        P(("expert", "dp"), None, None),
    )
    return jax.shard_map(
        per_device,
        mesh=mesh,
        in_specs=placed,
        out_specs=P(("groups", "expert", "dp"), None, None, None),
        check_vma=False,
    )
```

profile of v0, /device:TPU:0, one launch (start us, length us, event | category | flops | bytes accessed | tf_op | source)
XLA Modules:
  0.0 197.2 jit_solution(11601761072021900881)
XLA Ops:
  6.5 0.8 copy.36
  7.7 1.0 add.78
  8.6 1.9 add.79
  10.6 0.9 and.15
  11.4 1.9 and.16
  14.0 2.3 %sort.17 = (s32[32]{0:T(128)}, s32[32]{0:T(128)S(1)}) sort(s32[32]{0:T(128)} %param.17, s32[32]{0:T(128)S(1)} %iota.23), dimensions={0}, to_apply=%region_6.7 | sort | flops 160 | bytes 512 | tf_op jit(solution)/shard_map/jit(argsort)/sort | solution.py:77
  16.9 1.1 fusion.19
  18.0 2.8 %fusion.37 = (f32[32]{0:T(128)S(1)}, f32[32,2048]{1,0:T(8,128)S(1)}) fusion(pred[32,2048]{1,0:T(32,128)(4,1)S(1)} %fusion.19, bf16[2048,576]{1,0:T(8,128)(2,1)} %bitcast.39, bf16[32,1,576]{2,0,1:T(8,128)(2,1)} %param.13), kind=kOutput, calls=%fused_computation.51 | convolution fusion | flops 75694048 | bytes 2723968 | tf_op jit(solution)/shard_map/while/body/eval_jaxpr/dot_general | solution.py:29
  21.5 0.8 fusion.20
  22.3 1.7 fusion.11
  23.9 0.7 gather_fusion
  24.7 1.0 fusion.16
  26.6 0.9 convert_element_type.47
  27.5 1.2 dynamic-slice.2
  29.8 70.7 %all-reduce.3.cloned.1.call-done = f32[32,3584]{1,0:T(8,128)} async-done(((f32[32,3584]{1,0:T(8,128)}), f32[32,3584]{1,0:T(8,128)}) %all-reduce.3.cloned.1.call-update) | async-done | bytes 458768
  100.5 0.9 fusion.29
  102.2 13.2 %scatter_fusion = bf16[16,12,3584]{2,0,1:T(8,128)(2,1)S(1)} fusion(bf16[16,12,3584]{2,0,1:T(8,128)(2,1)S(1)} %broadcast_in_dim.70, s32[96]{0:T(128)S(1)} %get-tuple-element.19, bf16[96,3584]{1,0:T(8,128)(2,1)S(1)} %broadcast_bitcast_fusion), kind=kCustom, calls=%fused_computation.2 | custom fusion | bytes 2065152 | tf_op jit(solution)/shard_map/scatter | solution.py:107
  115.4 0.8 copy.38
  116.1 46.7 %all_to_all.10 = bf16[16,12,3584]{2,1,0:T(8,128)(2,1)S(1)} all-to-all(bf16[16,12,3584]{2,1,0:T(8,128)(2,1)S(1)} %copy.38), channel_id=1, replica_groups=mesh['groups'=2,'expert'=8,'dp'=2] {'expert','dp'}, dimensions={0} | all-to-all | bytes 2752512 | tf_op jit(solution)/shard_map/all_to_all | solution.py:112
  162.8 6.2 %multiply_convert_fusion = bf16[16,12,1024]{2,1,0:T(8,128)(2,1)} fusion(bf16[16,12,3584]{2,1,0:T(8,128)(2,1)S(1)} %all_to_all.10, bf16[1,3584,1024]{2,1,0:T(8,128)(2,1)} %param.25), kind=kOutput, calls=%fused_computation.12 | convolution fusion | flops 1410269184 | bytes 9109504 | tf_op jit(solution)/shard_map/scd,dh->sch/dot_general | solution.py:110
  169.0 4.0 %all-to-all-start.1 = ((bf16[16,12,1024]{2,1,0:T(8,128)(2,1)}), bf16[16,12,1024]{2,1,0:T(8,128)(2,1)S(1)}, u32[]{:S(2)}, u32[]{:S(2)}) async-start(bf16[16,12,1024]{2,1,0:T(8,128)(2,1)} %multiply_convert_fusion), calls=%async_computation.1 | async-start | bytes 1048576 | tf_op jit(solution)/shard_map/all_to_all | solution.py:116
  173.0 14.4 %all-to-all-done.1 = bf16[16,12,1024]{2,1,0:T(8,128)(2,1)S(1)} async-done(((bf16[16,12,1024]{2,1,0:T(8,128)(2,1)}), bf16[16,12,1024]{2,1,0:T(8,128)(2,1)S(1)}, u32[]{:S(2)}, u32[]{:S(2)}) %all-to-all-start.1) | async-done | bytes 393248 | tf_op jit(solution)/shard_map/all_to_all | solution.py:116
  187.7 1.9 gather_fusion.1
  189.6 0.8 fusion.18
  (42 shorter events, 4.5 us)
Async XLA Ops:
  6.5 18.1 %copy-start = (bf16[1,128,3584]{2,1,0:T(8,128)(2,1)S(1)}, bf16[1,128,3584]{2,1,0:T(8,128)(2,1)}, u32[]{:S(2)}) copy-start(bf16[1,128,3584]{2,1,0:T(8,128)(2,1)} %param.19) | copy-start | bytes 2752516
  6.5 94.0 %all-reduce.3.cloned.1.call-start = ((), (), s32[]{:S(2)}) async-start(), calls=%async_computation.2 | async-start | bytes 917504
  7.6 14.6 %copy-start.1 = (bf16[32,64,576]{2,1,0:T(8,128)(2,1)S(1)}, bf16[32,64,576]{2,1,0:T(8,128)(2,1)}, u32[]{:S(2)}) copy-start(bf16[32,64,576]{2,1,0:T(8,128)(2,1)} %param.14) | copy-start | bytes 7077892
  18.0 2.8 %copy-start.3 = (pred[32,2048]{1,0:T(32,128)(4,1)}, pred[32,2048]{1,0:T(32,128)(4,1)S(1)}, u32[]{:S(2)}) copy-start(pred[32,2048]{1,0:T(32,128)(4,1)S(1)} %fusion.19) | copy-start | bytes 196612
  20.8 0.7 copy-start.2
  20.8 0.7 copy-start.6
  22.3 5.2 %copy-start.4 = (bf16[3584]{0:T(1024)(128)(2,1)S(1)}, bf16[3584]{0:T(1024)(128)(2,1)}, u32[]{:S(2)}) copy-start(bf16[3584]{0:T(1024)(128)(2,1)} %param.22) | copy-start | bytes 21508
  162.8 10.2 %copy-start.5 = (f32[4,3,8]{2,0,1:T(4,128)S(1)}, f32[4,3,8]{2,0,1:T(4,128)}, u32[]{:S(2)}) copy-start(f32[4,3,8]{2,0,1:T(4,128)} %param.24) | copy-start | bytes 1156
  169.0 18.5 %all-to-all-start.1 = ((bf16[16,12,1024]{2,1,0:T(8,128)(2,1)}), bf16[16,12,1024]{2,1,0:T(8,128)(2,1)S(1)}, u32[]{:S(2)}, u32[]{:S(2)}) async-start(bf16[16,12,1024]{2,1,0:T(8,128)(2,1)} %multiply_convert_fusion), calls=%async_computation.1 | async-start | bytes 1048576 | tf_op jit(solution)/shard_map/all_to_all | solution.py:116
Sparse Core Ops, SparseCore 0:
  25.8 74.6 all-reduce.2
where the time goes:
time: 198 us; the launch traced here: 197 us
  waiting for transfers between devices  85.1 us (43%)
  blocking collectives  46.7 us (24%)
  local copies, waits for them, and re-layouts  27.2 us (14%)
  between operations  14.3 us (7%)
  matrix products  11.7 us (6%)
  other arithmetic  8.25 us (4%)
  starting transfers between devices  4.02 us (2%)
    unnamed x2, waiting for transfers between devices  70.7 us
    all_to_all x1, blocking collectives, per_device(): lax.all_to_all(outgoing, ('expert', 'dp'), split_axis=0, concat_axis=0, t...  46.7 us
    all_to_all x1, waiting for transfers between devices, per_device(): lax.all_to_all(jax.nn.silu(product).astype(jnp.bfloat16), ('expert', 'dp'...  14.4 us
    scatter x2, local copies, waits for them, and re-layouts, per_device(): outgoing = jnp.zeros((experts, capacity, D), jnp.bfloat16).at[route_flat,...  13.9 us
    dot_general x1, matrix products, per_device(): jnp.einsum('scd,dh->sch', lax.all_to_all(outgoing, ('expert', 'dp'), spli...  6.19 us
    all_to_all x1, starting transfers between devices, per_device(): lax.all_to_all(jax.nn.silu(product).astype(jnp.bfloat16), ('expert', 'dp'...  4.02 us
  transfers between devices with their start and end apart: 2, of which 2 were waited for; matrix products, arithmetic and copies ran while one was open for 2% of the time, Pallas kernels for 0%

commit v1 on v0

v1 whole, which is shorter than its diff:
```python
import functools

import jax
import jax.numpy as jnp
from jax import lax
from jax.experimental import pallas as pl
from jax.experimental.pallas import tpu as pltpu
from jax.sharding import PartitionSpec as P

LATENT = 512
ROPE = 64
VHEAD = 128
VERIFY = 3
BF = jnp.bfloat16
F32 = jnp.float32
VMEM = pl.BlockSpec(memory_space=pltpu.VMEM)


def params(mib=40):
    return pltpu.CompilerParams(vmem_limit_bytes=mib * 1024 * 1024)


def as_column(row, size):
    eye = lax.broadcasted_iota(jnp.int32, (size, size), 0) == lax.broadcasted_iota(
        jnp.int32, (size, size), 1
    )
    return jnp.sum(jnp.where(eye, row, 0), axis=1, keepdims=True)


def attention_kernel(per_owner, q_ref, kv_ref, table_ref, length_ref, owner_ref, up_ref, out_ref, sum_ref):
    rows = q_ref.shape[0]
    tokens = kv_ref.shape[0]
    slots = table_ref.shape[0]
    page_len = 64
    token = lax.broadcasted_iota(jnp.int32, (1, tokens), 1)
    page, offset = token // page_len, token % page_len
    position = jnp.full((rows, tokens), 1 << 24, jnp.int32)
    for slot in range(slots):
        named = as_column(table_ref[slot : slot + 1, :], rows)
        position = jnp.where(named == page, slot * page_len + offset, position)
    visible = position < as_column(length_ref[...], rows)
    scores = lax.dot_general(
        q_ref[...], kv_ref[...], (((1,), (1,)), ((), ())), preferred_element_type=F32
    ) * (VHEAD + ROPE) ** (-0.5)
    masked = jnp.where(visible, scores, -1e30)
    row_max = jnp.max(masked, axis=1, keepdims=True)
    exponent = jnp.where(visible, jnp.exp(masked - row_max), 0.0)
    attention = (exponent / jnp.sum(exponent, axis=1, keepdims=True)).astype(BF)
    context = jnp.dot(attention, kv_ref[:, :LATENT], preferred_element_type=F32).astype(BF)
    values = jnp.dot(context, up_ref[...], preferred_element_type=F32).astype(BF)
    owner = owner_ref[...]
    first = lax.broadcasted_iota(jnp.int32, (rows, rows), 0)
    second = lax.broadcasted_iota(jnp.int32, (rows, rows), 1)
    before = (as_column(owner, rows) == owner) & (first < second)
    target = owner * per_owner + jnp.sum(before.astype(jnp.int32), axis=0, keepdims=True)
    picked = jnp.dot((first == target).astype(BF), values, preferred_element_type=F32).astype(BF)
    summed = jnp.dot(picked, out_ref[...], preferred_element_type=F32).astype(BF)
    for e in range(rows // per_owner):
        sum_ref[e] = summed[e * per_owner : (e + 1) * per_owner]


def normed(states, gain):
    scale = lax.rsqrt(jnp.mean(states * states, axis=-1, keepdims=True) + 1e-06)
    return (states * scale * gain).astype(BF)


def norm_verify_kernel(states_ref, gain_ref, out_ref):
    gain = gain_ref[...].astype(F32)
    count = states_ref.shape[1]
    rows = [
        normed(states_ref[q].astype(F32), gain) for q in range(states_ref.shape[0])
    ]
    out_ref[...] = jnp.concatenate(rows, axis=0)


def norm_draft_kernel(copies, parts_ref, residual_ref, gain_ref, out_ref):
    states = residual_ref[...].astype(F32)
    total = parts_ref[0].astype(F32)
    for e in range(1, parts_ref.shape[0]):
        total = total + parts_ref[e].astype(F32)
    tokens = normed(states + total, gain_ref[...].astype(F32))
    for c in range(copies):
        out_ref[c] = tokens


def expert_kernel(codes, verify_ref, draft_ref, weight_ref, out_ref):
    me = lax.axis_index("expert") * lax.axis_size("dp") + lax.axis_index("dp")
    devices, per_draft, width = draft_ref.shape
    weight = weight_ref[...]
    product = jnp.dot(verify_ref[...], weight, preferred_element_type=F32)
    active = (product * jax.nn.sigmoid(product)).astype(BF)
    per_verify = active.shape[0] // devices
    for block, code in enumerate(codes):
        out_ref[me ^ code, per_draft:] = active[block * per_verify : (block + 1) * per_verify]
    draft = draft_ref[...].reshape(devices * per_draft, width)
    product = jnp.dot(draft, weight, preferred_element_type=F32)
    active = (product * jax.nn.sigmoid(product)).astype(BF)
    for d in range(devices):
        out_ref[d, :per_draft] = active[d * per_draft : (d + 1) * per_draft]


def select_kernel(order, ids_ref, gates_ref, back_ref, out_ref):
    devices, per, width = back_ref.shape
    top = ids_ref.shape[2]
    eye = lax.broadcasted_iota(jnp.int32, (top, top), 0) == lax.broadcasted_iota(
        jnp.int32, (top, top), 1
    )
    source = lax.broadcasted_iota(jnp.int32, (top, devices), 1)
    for t in range(ids_ref.shape[0]):
        for q in range(ids_ref.shape[1]):
            ids = jnp.sum(jnp.where(eye, ids_ref[t, q : q + 1, :], 0), axis=1, keepdims=True)
            gates = jnp.sum(
                jnp.where(eye, gates_ref[t, q : q + 1, :], 0.0), axis=1, keepdims=True
            )
            chosen = (ids == source).astype(BF)
            rows = back_ref[:, order(q, t), :]
            active = jnp.dot(chosen, rows, preferred_element_type=F32)
            out_ref[q, t] = (gates * active).astype(BF)


def swap(x, axis, size, mask):
    return lax.ppermute(x, axis, [(i, i ^ mask) for i in range(size)])


def per_device(queries, kv_pages, page_tables, lengths, owners, up_values, out_proj, residual,
               verify_states, norm_gain, route_ids, route_weights, expert_up):
    rows, _, key_width = queries.shape
    verify_rows, width = residual.shape
    n_expert, n_dp = lax.axis_size("expert"), lax.axis_size("dp")
    experts = n_expert * n_dp
    hidden = expert_up.shape[2]
    gain = norm_gain.reshape(1, width)

    verify_tokens = pl.pallas_call(
        norm_verify_kernel,
        out_shape=jax.ShapeDtypeStruct((verify_rows * (VERIFY - 1), width), BF),
        in_specs=[VMEM, VMEM],
        out_specs=VMEM,
        name="norm_verify",
        compiler_params=params(),
    )(verify_states, gain)

    partial_sums = pl.pallas_call(
        functools.partial(attention_kernel, verify_rows),
        out_shape=jax.ShapeDtypeStruct((n_expert, verify_rows, width), BF),
        in_specs=[VMEM] * 7,
        out_specs=VMEM,
        name="attention",
        compiler_params=params(),
    )(
        queries.reshape(rows, key_width),
        kv_pages.reshape(-1, key_width),
        page_tables.T,
        lengths.reshape(1, rows),
        owners.reshape(1, rows),
        up_values[0],
        out_proj[0],
    )

    gathered = verify_tokens
    codes = [0]
    mask = n_expert // 2
    while mask:
        gathered = jnp.concatenate([gathered, swap(gathered, "expert", n_expert, mask)], axis=0)
        codes += [code ^ (mask * n_dp) for code in codes]
        mask //= 2
    gathered = jnp.concatenate([gathered, swap(gathered, "dp", n_dp, 1)], axis=0)
    codes += [code ^ 1 for code in codes]

    parts = lax.all_to_all(partial_sums, "expert", split_axis=0, concat_axis=0, tiled=True)
    draft_tokens = pl.pallas_call(
        functools.partial(norm_draft_kernel, experts),
        out_shape=jax.ShapeDtypeStruct((experts, verify_rows, width), BF),
        in_specs=[VMEM] * 3,
        out_specs=VMEM,
        name="norm_draft",
        compiler_params=params(),
    )(parts, residual, gain)
    draft = lax.all_to_all(draft_tokens, ("expert", "dp"), split_axis=0, concat_axis=0, tiled=True)
    active = pl.pallas_call(
        functools.partial(expert_kernel, codes),
        out_shape=jax.ShapeDtypeStruct((experts, verify_rows * VERIFY, hidden), BF),
        in_specs=[VMEM] * 3,
        out_specs=VMEM,
        name="expert",
        compiler_params=params(),
    )(gathered, draft, expert_up[0])
    back = lax.all_to_all(active, ("expert", "dp"), split_axis=0, concat_axis=0, tiled=True)
    top = route_ids.shape[2]

    def order(q, t):
        return q if t == 0 else verify_rows + q * (VERIFY - 1) + t - 1

    return pl.pallas_call(
        functools.partial(select_kernel, order),
        out_shape=jax.ShapeDtypeStruct((verify_rows, VERIFY, top, hidden), BF),
        in_specs=[VMEM] * 3,
        out_specs=VMEM,
        name="select",
        compiler_params=params(),
    )(route_ids.transpose(1, 0, 2), route_weights.transpose(1, 0, 2), back)


def solution(mesh):
    placed = (
        P(("groups", "dp"), "expert", None),
        P(("groups", "dp"), None, None),
        P(("groups", "dp"), None),
        P(("groups", "dp")),
        P(("groups", "dp")),
        P("expert", None, None),
        P("expert", None, None),
        P(("groups", "expert", "dp"), None),
        P(("groups", "expert", "dp"), None, None),
        P(),
        P(("groups", "expert", "dp"), None, None),
        P(("groups", "expert", "dp"), None, None),
        P(("expert", "dp"), None, None),
    )
    return jax.shard_map(
        per_device,
        mesh=mesh,
        in_specs=placed,
        out_specs=P(("groups", "expert", "dp"), None, None, None),
        check_vma=False,
    )
```

time: 198 us -> 79.6 us (0.40)
  waiting for transfers between devices: 85.1 us -> 24.1 us
  blocking collectives: 46.7 us -> 18.2 us
  local copies, waits for them, and re-layouts: 27.2 us -> 12 us
  between operations: 14.3 us -> 0.13 us
  starting transfers between devices: 4.02 us -> 16.7 us
  matrix products: 11.7 us -> 0 us
  other arithmetic: 8.25 us -> 0.07 us
  Pallas kernels: 0 us -> 7.62 us
    unnamed x2 -> x0, waiting for transfers between devices: 70.7 us -> none
    all_to_all x1, blocking collectives: 46.7 us -> 18.2 us  [per_device(): lax.all_to_all(active, ('expert', 'dp'), split_axis=0, concat_axis=0, til...]
    scatter x2 -> x0, local copies, waits for them, and re-layouts: 13.9 us -> none  [per_device(): outgoing = jnp.zeros((experts, capacity, D), jnp.bfloat16).at[route_flat,...]
    dot_general x4 -> x0, matrix products: 11.7 us -> none  [the longest x1 6.19 us: per_device(): jnp.einsum('scd,dh->sch', lax.all_to_all(outgoing, ('expert', 'dp'), spli...]
    ppermute x0 -> x4, waiting for transfers between devices: none -> 11 us  [swap(): return lax.ppermute(x, axis, [(i, i ^ mask) for i in range(size)])]
    unnamed x18 -> x28, local copies, waits for them, and re-layouts: 3.49 us -> 11.3 us
    pallas_call x0 -> x5, Pallas kernels: none -> 7.62 us  [the longest x1 2.71 us: per_device(): pl.pallas_call(functools.partial(attention_kernel, verify_rows), out_shap...]
    ppermute x0 -> x4, starting transfers between devices: none -> 7.47 us  [swap(): return lax.ppermute(x, axis, [(i, i ^ mask) for i in range(size)])]
  transfers between devices with their start and end apart: 2 -> 6, of which waited for: 2 -> 3; matrix products, arithmetic and copies ran while one was open for 2% -> 0% of each run, Pallas kernels for 0% -> 5%
where the time goes in v1:
time: 79.6 us; the launch traced here: 78.9 us
  waiting for transfers between devices  24.1 us (30%)
  blocking collectives  18.2 us (23%)
  starting transfers between devices  16.7 us (21%)
  local copies, waits for them, and re-layouts  12 us (15%)
  Pallas kernels  7.62 us (10%)
    all_to_all x1, blocking collectives, per_device(): lax.all_to_all(active, ('expert', 'dp'), split_axis=0, concat_axis=0, til...  18.2 us
    all_to_all x1, waiting for transfers between devices, per_device(): lax.all_to_all(draft_tokens, ('expert', 'dp'), split_axis=0, concat_axis=...  13.2 us
    unnamed x28, local copies, waits for them, and re-layouts  11.3 us
    ppermute x4, waiting for transfers between devices, swap(): return lax.ppermute(x, axis, [(i, i ^ mask) for i in range(size)])  11 us
    ppermute x4, starting transfers between devices, swap(): return lax.ppermute(x, axis, [(i, i ^ mask) for i in range(size)])  7.47 us
    all_to_all x1, starting transfers between devices, per_device(): lax.all_to_all(draft_tokens, ('expert', 'dp'), split_axis=0, concat_axis=...  5.5 us
    all_to_all x1, starting transfers between devices, per_device(): lax.all_to_all(partial_sums, 'expert', split_axis=0, concat_axis=0, tiled...  3.78 us
    pallas_call x1, Pallas kernels, per_device(): pl.pallas_call(functools.partial(attention_kernel, verify_rows), out_shap...  2.71 us
  transfers between devices with their start and end apart: 6, of which 3 were waited for; matrix products, arithmetic and copies ran while one was open for 0% of the time, Pallas kernels for 5%

profile of v1, /device:TPU:0, one launch (start us, length us, event | category | flops | bytes accessed | tf_op | source)
XLA Modules:
  0.0 78.9 jit_solution(11203775363120474496)
XLA Ops:
  0.0 0.7 reshape.15.gain_ref
  0.7 0.8 %copy-done.4 = bf16[4,2,3584]{2,1,0:T(2,128)(2,1)S(1)} copy-done((bf16[4,2,3584]{2,1,0:T(2,128)(2,1)S(1)}, bf16[4,2,3584]{2,1,0:T(2,128)(2,1)}, u32[]{:S(2)}) %copy-start.4) | copy-done | bytes 57368
  1.7 4.1 %collective-permute-start = (bf16[8,3584]{1,0:T(8,128)(2,1)S(1)}, bf16[8,3584]{1,0:T(8,128)(2,1)S(1)}, u32[]{:S(2)}, u32[]{:S(2)}) collective-permute-start(bf16[8,3584]{1,0:T(8,128)(2,1)S(1)} %norm_verify.1), channel_id=1, source_target_pairs={{0,8},{2,10},{4,12},{6,14},{8,0},{10,2},{12,4},{14,6},{1,9},{3,11}... | collective-permute-start | bytes 172040 | tf_op jit(solution)/shard_map/ppermute | solution.py:122
  5.8 1.7 %copy-done.1 = bf16[32,64,576]{2,1,0:T(8,128)(2,1)S(1)} copy-done((bf16[32,64,576]{2,1,0:T(8,128)(2,1)S(1)}, bf16[32,64,576]{2,1,0:T(8,128)(2,1)}, u32[]{:S(2)}) %copy-start.1) | copy-done | bytes 2359320
  7.6 1.2 %copy-done.2 = bf16[1,128,3584]{2,1,0:T(8,128)(2,1)S(1)} copy-done((bf16[1,128,3584]{2,1,0:T(8,128)(2,1)S(1)}, bf16[1,128,3584]{2,1,0:T(8,128)(2,1)}, u32[]{:S(2)}) %copy-start.2) | copy-done | bytes 917528
  8.7 0.9 %copy-done.3 = bf16[1,512,128]{2,1,0:T(8,128)(2,1)S(1)} copy-done((bf16[1,512,128]{2,1,0:T(8,128)(2,1)S(1)}, bf16[1,512,128]{2,1,0:T(8,128)(2,1)}, u32[]{:S(2)}) %copy-start.3) | copy-done | bytes 131096
  9.7 0.8 copy-done.5
  10.4 0.7 copy-done.9
  11.1 0.7 copy-done.10
  11.8 0.7 copy-done.11
  12.4 2.7 %attention.1 = bf16[8,4,3584]{2,1,0:T(4,128)(2,1)} custom-call(bf16[32,576]{1,0:T(8,128)(2,1)S(1)} %bitcast.14, bf16[2048,576]{1,0:T(8,128)(2,1)S(1)} %bitcast.11, s32[8,32]{1,0:T(8,128)S(1)} %bitcast.17, s32[1,32]{1,0:T(1,128)S(1)} %bitcast.18, s32[1,32]{1,0:T(1,128)S(1)} %bitcast.19, bf16[512,128]{1,0:T(8,128)(2,1)S(1)} %bitcast.13, ...), custom_call_target="tpu_custom_call" | custom-call | tf_op jit(solution)/shard_map/attention/pallas_call | solution.py:143
  15.1 3.8 %all-to-all-start = ((bf16[8,4,3584]{2,1,0:T(4,128)(2,1)}), bf16[8,4,3584]{2,1,0:T(4,128)(2,1)S(1)}, u32[]{:S(2)}, u32[]{:S(2)}) async-start(bf16[8,4,3584]{2,1,0:T(4,128)(2,1)} %attention.1), calls=%async_computation | async-start | bytes 458752 | tf_op jit(solution)/shard_map/all_to_all | solution.py:170
  18.9 2.1 %collective-permute-start.1 = (bf16[16,3584]{1,0:T(8,128)(2,1)S(1)}, bf16[16,3584]{1,0:T(8,128)(2,1)S(1)}, u32[]{:S(2)}, u32[]{:S(2)}) collective-permute-start(bf16[16,3584]{1,0:T(8,128)(2,1)S(1)} %pad_maximum_fusion.2), channel_id=1, source_target_pairs={{0,4},{2,6},{4,0},{6,2},{8,12},{10,14},{12,8},{14,10},{1,5},{3,7},... | collective-permute-start | bytes 344072 | tf_op jit(solution)/shard_map/ppermute | solution.py:122
  21.0 6.1 %collective-permute-done.1 = bf16[16,3584]{1,0:T(8,128)(2,1)S(1)} collective-permute-done((bf16[16,3584]{1,0:T(8,128)(2,1)S(1)}, bf16[16,3584]{1,0:T(8,128)(2,1)S(1)}, u32[]{:S(2)}, u32[]{:S(2)}) %collective-permute-start.1) | collective-permute-done | bytes 114720 | tf_op jit(solution)/shard_map/ppermute | solution.py:122
  27.2 1.2 %collective-permute-start.2 = (bf16[32,3584]{1,0:T(8,128)(2,1)S(1)}, bf16[32,3584]{1,0:T(8,128)(2,1)S(1)}, u32[]{:S(2)}, u32[]{:S(2)}) collective-permute-start(bf16[32,3584]{1,0:T(8,128)(2,1)S(1)} %pad_maximum_fusion.1), channel_id=1, source_target_pairs={{0,2},{2,0},{4,6},{6,4},{8,10},{10,8},{12,14},{14,12},{1,3},{3,1},... | collective-permute-start | bytes 688136 | tf_op jit(solution)/shard_map/ppermute | solution.py:122
  28.4 4.9 %collective-permute-done.2 = bf16[32,3584]{1,0:T(8,128)(2,1)S(1)} collective-permute-done((bf16[32,3584]{1,0:T(8,128)(2,1)S(1)}, bf16[32,3584]{1,0:T(8,128)(2,1)S(1)}, u32[]{:S(2)}, u32[]{:S(2)}) %collective-permute-start.2) | collective-permute-done | bytes 229408 | tf_op jit(solution)/shard_map/ppermute | solution.py:122
  33.4 0.7 copy-done.6
  34.2 0.9 %norm_draft.1 = bf16[16,4,3584]{2,1,0:T(4,128)(2,1)} custom-call(bf16[8,4,3584]{2,1,0:T(4,128)(2,1)S(1)} %all-to-all-done.parts_ref, bf16[4,3584]{1,0:T(4,128)(2,1)S(1)} %copy-done.6, bf16[1,3584]{1,0:T(2,128)(2,1)S(1)} %reshape.15.gain_ref), custom_call_target="tpu_custom_call" | custom-call | tf_op jit(solution)/shard_map/norm_draft/pallas_call | solution.py:171
  35.1 5.5 %all-to-all-start.1 = ((bf16[16,4,3584]{2,1,0:T(4,128)(2,1)}), bf16[16,4,3584]{2,1,0:T(4,128)(2,1)S(1)}, u32[]{:S(2)}, u32[]{:S(2)}) async-start(bf16[16,4,3584]{2,1,0:T(4,128)(2,1)} %norm_draft.1), calls=%async_computation.1 | async-start | bytes 917504 | tf_op jit(solution)/shard_map/all_to_all | solution.py:179
  40.7 13.2 %all-to-all-done.1.draft_ref = bf16[16,4,3584]{2,1,0:T(4,128)(2,1)S(1)} async-done(((bf16[16,4,3584]{2,1,0:T(4,128)(2,1)}), bf16[16,4,3584]{2,1,0:T(4,128)(2,1)S(1)}, u32[]{:S(2)}, u32[]{:S(2)}) %all-to-all-start.1) | async-done | bytes 458784 | tf_op jit(solution)/shard_map/all_to_all | solution.py:179
  53.9 3.1 %copy-done = bf16[1,3584,1024]{2,1,0:T(8,128)(2,1)S(1)} copy-done((bf16[1,3584,1024]{2,1,0:T(8,128)(2,1)S(1)}, bf16[1,3584,1024]{2,1,0:T(8,128)(2,1)}, u32[]{:S(2)}) %copy-start) | copy-done | bytes 7340056
  56.9 2.4 %expert.1 = bf16[16,12,1024]{2,1,0:T(8,128)(2,1)S(1)} custom-call(bf16[128,3584]{1,0:T(8,128)(2,1)S(1)} %constant_dynamic-update-slice_fusion.verify_ref, bf16[16,4,3584]{2,1,0:T(4,128)(2,1)S(1)} %all-to-all-done.1.draft_ref, bf16[3584,1024]{1,0:T(8,128)(2,1)S(1)} %bitcast.10), custom_call_target="tpu_custom_call" | custom-call | tf_op jit(solution)/shard_map/expert/pallas_call | solution.py:180
  59.3 18.2 %all_to_all.15.back_ref = bf16[16,12,1024]{2,1,0:T(8,128)(2,1)S(1)} all-to-all(bf16[16,12,1024]{2,1,0:T(8,128)(2,1)S(1)} %expert.1), channel_id=1, replica_groups=mesh['groups'=2,'expert'=8,'dp'=2] {'expert','dp'}, dimensions={0} | all-to-all | bytes 786432 | tf_op jit(solution)/shard_map/all_to_all | solution.py:188
  77.5 1.4 %select.1 = bf16[4,3,8,1024]{3,2,1,0:T(8,128)(2,1)} custom-call(s32[3,4,8]{2,1,0:T(4,128)S(1)} %bitcast.15, f32[3,4,8]{2,1,0:T(4,128)S(1)} %bitcast.16, bf16[16,12,1024]{2,1,0:T(8,128)(2,1)S(1)} %all_to_all.15.back_ref), custom_call_target="tpu_custom_call" | custom-call | tf_op jit(solution)/shard_map/select/pallas_call | solution.py:194
  (27 shorter events, 0.4 us)
Async XLA Ops:
  0.7 0.8 %copy-start.4 = (bf16[4,2,3584]{2,1,0:T(2,128)(2,1)S(1)}, bf16[4,2,3584]{2,1,0:T(2,128)(2,1)}, u32[]{:S(2)}) copy-start(bf16[4,2,3584]{2,1,0:T(2,128)(2,1)} %states_ref.1) | copy-start | bytes 172036
  1.7 17.2 %collective-permute-start = (bf16[8,3584]{1,0:T(8,128)(2,1)S(1)}, bf16[8,3584]{1,0:T(8,128)(2,1)S(1)}, u32[]{:S(2)}, u32[]{:S(2)}) collective-permute-start(bf16[8,3584]{1,0:T(8,128)(2,1)S(1)} %norm_verify.1), channel_id=1, source_target_pairs={{0,8},{2,10},{4,12},{6,14},{8,0},{10,2},{12,4},{14,6},{1,9},{3,11}... | collective-permute-start | bytes 172040 | tf_op jit(solution)/shard_map/ppermute | solution.py:122
  5.8 1.7 %copy-start.1 = (bf16[32,64,576]{2,1,0:T(8,128)(2,1)S(1)}, bf16[32,64,576]{2,1,0:T(8,128)(2,1)}, u32[]{:S(2)}) copy-start(bf16[32,64,576]{2,1,0:T(8,128)(2,1)} %param.14) | copy-start | bytes 7077892
  7.6 1.2 %copy-start.2 = (bf16[1,128,3584]{2,1,0:T(8,128)(2,1)S(1)}, bf16[1,128,3584]{2,1,0:T(8,128)(2,1)}, u32[]{:S(2)}) copy-start(bf16[1,128,3584]{2,1,0:T(8,128)(2,1)} %param.19) | copy-start | bytes 2752516
  8.7 0.9 %copy-start.3 = (bf16[1,512,128]{2,1,0:T(8,128)(2,1)S(1)}, bf16[1,512,128]{2,1,0:T(8,128)(2,1)}, u32[]{:S(2)}) copy-start(bf16[1,512,128]{2,1,0:T(8,128)(2,1)} %param.18) | copy-start | bytes 393220
  9.7 0.8 copy-start.5
  10.4 0.7 copy-start.9
  11.1 0.7 copy-start.10
  11.8 0.7 copy-start.11
  15.1 18.3 %all-to-all-start = ((bf16[8,4,3584]{2,1,0:T(4,128)(2,1)}), bf16[8,4,3584]{2,1,0:T(4,128)(2,1)S(1)}, u32[]{:S(2)}, u32[]{:S(2)}) async-start(bf16[8,4,3584]{2,1,0:T(4,128)(2,1)} %attention.1), calls=%async_computation | async-start | bytes 458752 | tf_op jit(solution)/shard_map/all_to_all | solution.py:170
  18.9 8.2 %collective-permute-start.1 = (bf16[16,3584]{1,0:T(8,128)(2,1)S(1)}, bf16[16,3584]{1,0:T(8,128)(2,1)S(1)}, u32[]{:S(2)}, u32[]{:S(2)}) collective-permute-start(bf16[16,3584]{1,0:T(8,128)(2,1)S(1)} %pad_maximum_fusion.2), channel_id=1, source_target_pairs={{0,4},{2,6},{4,0},{6,2},{8,12},{10,14},{12,8},{14,10},{1,5},{3,7},... | collective-permute-start | bytes 344072 | tf_op jit(solution)/shard_map/ppermute | solution.py:122
  27.2 50.3 %copy-start.7 = (s32[4,3,8]{2,0,1:T(4,128)S(1)}, s32[4,3,8]{2,0,1:T(4,128)}, u32[]{:S(2)}) copy-start(s32[4,3,8]{2,0,1:T(4,128)} %param.23) | copy-start | bytes 1156
  27.2 50.3 %copy-start.8 = (f32[4,3,8]{2,0,1:T(4,128)S(1)}, f32[4,3,8]{2,0,1:T(4,128)}, u32[]{:S(2)}) copy-start(f32[4,3,8]{2,0,1:T(4,128)} %param.24) | copy-start | bytes 1156
  27.2 6.1 %collective-permute-start.2 = (bf16[32,3584]{1,0:T(8,128)(2,1)S(1)}, bf16[32,3584]{1,0:T(8,128)(2,1)S(1)}, u32[]{:S(2)}, u32[]{:S(2)}) collective-permute-start(bf16[32,3584]{1,0:T(8,128)(2,1)S(1)} %pad_maximum_fusion.1), channel_id=1, source_target_pairs={{0,2},{2,0},{4,6},{6,4},{8,10},{10,8},{12,14},{14,12},{1,3},{3,1},... | collective-permute-start | bytes 688136 | tf_op jit(solution)/shard_map/ppermute | solution.py:122
  33.3 7.3 %collective-permute-start.3 = (bf16[64,3584]{1,0:T(8,128)(2,1)S(1)}, bf16[64,3584]{1,0:T(8,128)(2,1)S(1)}, u32[]{:S(2)}, u32[]{:S(2)}) collective-permute-start(bf16[64,3584]{1,0:T(8,128)(2,1)S(1)} %pad_maximum_fusion), channel_id=1, source_target_pairs={{0,1},{1,0},{2,3},{3,2},{4,5},{5,4},{6,7},{7,6},{8,9},{9,8},{10,11... | collective-permute-start | bytes 1376264 | tf_op jit(solution)/shard_map/ppermute | solution.py:122
  33.4 0.8 copy-start.6
  35.1 18.8 %all-to-all-start.1 = ((bf16[16,4,3584]{2,1,0:T(4,128)(2,1)}), bf16[16,4,3584]{2,1,0:T(4,128)(2,1)S(1)}, u32[]{:S(2)}, u32[]{:S(2)}) async-start(bf16[16,4,3584]{2,1,0:T(4,128)(2,1)} %norm_draft.1), calls=%async_computation.1 | async-start | bytes 917504 | tf_op jit(solution)/shard_map/all_to_all | solution.py:179
  53.9 3.1 %copy-start = (bf16[1,3584,1024]{2,1,0:T(8,128)(2,1)S(1)}, bf16[1,3584,1024]{2,1,0:T(8,128)(2,1)}, u32[]{:S(2)}) copy-start(bf16[1,3584,1024]{2,1,0:T(8,128)(2,1)} %param.25) | copy-start | bytes 22020100

commit v2 on v1

v2 whole, which is shorter than its diff:
```python
import functools

import jax
import jax.numpy as jnp
from jax import lax
from jax.experimental import pallas as pl
from jax.experimental.pallas import tpu as pltpu
from jax.sharding import PartitionSpec as P

LATENT = 512
ROPE = 64
VHEAD = 128
VERIFY = 3
PAGES = 32
NEAR = 2
CHUNKS = 7
ROW_BLOCK = 256
BF = jnp.bfloat16
F32 = jnp.float32
VMEM = pl.BlockSpec(memory_space=pltpu.VMEM)
HBM = pl.BlockSpec(memory_space=pltpu.HBM)


def params(mib=40):
    return pltpu.CompilerParams(vmem_limit_bytes=mib * 1024 * 1024)


def as_column(row, size):
    eye = lax.broadcasted_iota(jnp.int32, (size, size), 0) == lax.broadcasted_iota(
        jnp.int32, (size, size), 1
    )
    return jnp.sum(jnp.where(eye, row, 0), axis=1, keepdims=True)


def fetch(sources, targets, semaphores):
    copies = [
        pltpu.make_async_copy(source, target, semaphores.at[i])
        for i, (source, target) in enumerate(zip(sources, targets))
    ]
    for copy in copies:
        copy.start()
    return copies


def attention_kernel(per_owner, *refs):
    sources, sum_ref, targets, semaphores = refs[:7], refs[7], refs[8:15], refs[15]
    copies = fetch(sources, targets, semaphores)
    q_ref, kv_ref, table_ref, length_ref, owner_ref, up_ref, out_ref = targets
    rows = q_ref.shape[0]
    tokens = kv_ref.shape[0]
    slots = table_ref.shape[0]
    page_len = tokens // PAGES
    token = lax.broadcasted_iota(jnp.int32, (1, tokens), 1)
    page, offset = token // page_len, token % page_len
    position = jnp.full((rows, tokens), 1 << 24, jnp.int32)
    for copy in copies[2:5]:
        copy.wait()
    for slot in range(slots):
        named = as_column(table_ref[slot : slot + 1, :], rows)
        position = jnp.where(named == page, slot * page_len + offset, position)
    visible = position < as_column(length_ref[...], rows)
    owner = owner_ref[...]
    first = lax.broadcasted_iota(jnp.int32, (rows, rows), 0)
    second = lax.broadcasted_iota(jnp.int32, (rows, rows), 1)
    before = (as_column(owner, rows) == owner) & (first < second)
    target = owner * per_owner + jnp.sum(before.astype(jnp.int32), axis=0, keepdims=True)
    for copy in copies[:2]:
        copy.wait()
    scores = lax.dot_general(
        q_ref[...], kv_ref[...], (((1,), (1,)), ((), ())), preferred_element_type=F32
    ) * (VHEAD + ROPE) ** (-0.5)
    masked = jnp.where(visible, scores, -1e30)
    row_max = jnp.max(masked, axis=1, keepdims=True)
    exponent = jnp.where(visible, jnp.exp(masked - row_max), 0.0)
    attention = (exponent / jnp.sum(exponent, axis=1, keepdims=True)).astype(BF)
    context = jnp.dot(attention, kv_ref[:, :LATENT], preferred_element_type=F32).astype(BF)
    for copy in copies[5:]:
        copy.wait()
    values = jnp.dot(context, up_ref[...], preferred_element_type=F32).astype(BF)
    picked = jnp.dot((first == target).astype(BF), values, preferred_element_type=F32).astype(BF)
    summed = jnp.dot(picked, out_ref[...], preferred_element_type=F32).astype(BF)
    groups, per_group, _ = sum_ref.shape
    for e in range(groups):
        sum_ref[e] = summed[e * per_group : (e + 1) * per_group]


def normed(states, gain):
    scale = lax.rsqrt(jnp.mean(states * states, axis=-1, keepdims=True) + 1e-06)
    return (states * scale * gain).astype(BF)


def far_sum_kernel(parts_ref, residual_ref, out_ref):
    total = parts_ref[0].astype(F32)
    for e in range(1, parts_ref.shape[0]):
        total = total + parts_ref[e].astype(F32)
    residual = residual_ref[...].astype(F32)
    rows = residual.shape[0]
    near = lax.rem(lax.axis_index("expert"), NEAR)
    twice = jnp.concatenate([residual] * NEAR, axis=0)
    place = lax.broadcasted_iota(jnp.int32, twice.shape, 0) // rows
    out_ref[...] = (total + jnp.where(place == near, twice, 0.0)).astype(BF)


def norm_draft_kernel(mine_ref, theirs_ref, gain_ref, out_ref):
    states = mine_ref[...].astype(F32) + theirs_ref[...].astype(F32)
    tokens = normed(states, gain_ref[...])
    for c in range(out_ref.shape[0]):
        out_ref[c] = tokens


def expert_kernel(codes, draft_ref, draft_other_ref, verify_ref, verify_other_ref, gain_ref, weight_hbm, out_ref,
                  weight_ref, tokens_ref, semaphores):
    chunks = semaphores.shape[0]
    depth = weight_ref.shape[0] // chunks
    copies = [
        pltpu.make_async_copy(
            weight_hbm.at[pl.ds(i * depth, depth)], weight_ref.at[pl.ds(i * depth, depth)], semaphores.at[i]
        )
        for i in range(chunks)
    ]
    for copy in copies:
        copy.start()
    n_dp = lax.axis_size("dp")
    dp = lax.axis_index("dp")
    me = lax.axis_index("expert") * n_dp + dp
    groups, per_group, width = draft_ref.shape
    per = out_ref.shape[2]
    rows = groups * per_group
    tokens_ref[:rows] = draft_ref[...].reshape(rows, width)
    tokens_ref[rows : 2 * rows] = draft_other_ref[...].reshape(rows, width)
    gain = gain_ref[...].astype(F32)
    half = verify_ref.shape[0]
    for part, states_ref in enumerate((verify_ref, verify_other_ref)):
        for start in range(0, half, ROW_BLOCK):
            stop = min(start + ROW_BLOCK, half)
            place = 2 * rows + part * half
            tokens_ref[place + start : place + stop] = normed(states_ref[start:stop].astype(F32), gain)
    total = tokens_ref.shape[0]
    for first in range(0, total, ROW_BLOCK):
        last = min(first + ROW_BLOCK, total)
        product = 0.0
        for i, copy in enumerate(copies):
            if first == 0:
                copy.wait()
            part = slice(i * depth, (i + 1) * depth)
            product = product + jnp.dot(
                tokens_ref[first:last, part], weight_ref[part], preferred_element_type=F32
            )
        active = (product * jax.nn.sigmoid(product)).astype(BF)
        for unit in range(first // per, last // per):
            if unit * per < 2 * rows:
                part, e = divmod(unit, rows // per)
                target, t = n_dp * e + (dp ^ part), 0
            else:
                block, t = divmod(unit - 2 * rows // per, VERIFY - 1)
                target, t = me ^ codes[block], t + 1
            out_ref[target, t] = active[unit * per - first : unit * per - first + per]


def select_kernel(ids_ref, gates_ref, back_ref, out_ref):
    devices, _, per, _ = back_ref.shape
    top = ids_ref.shape[2]
    eye = lax.broadcasted_iota(jnp.int32, (top, top), 0) == lax.broadcasted_iota(
        jnp.int32, (top, top), 1
    )
    source = lax.broadcasted_iota(jnp.int32, (top, devices), 1)
    for t in range(ids_ref.shape[0]):
        for q in range(ids_ref.shape[1]):
            ids = jnp.sum(jnp.where(eye, ids_ref[t, q : q + 1, :], 0), axis=1, keepdims=True)
            gates = jnp.sum(
                jnp.where(eye, gates_ref[t, q : q + 1, :], 0.0), axis=1, keepdims=True
            )
            chosen = (ids == source).astype(BF)
            place = q if t == 0 else per + q * (VERIFY - 1) + t - 1
            rows = back_ref[:, place // per, place % per, :]
            active = jnp.dot(chosen, rows, preferred_element_type=F32)
            out_ref[q, t] = (gates * active).astype(BF)


def swap(x, axis, size, mask):
    return lax.ppermute(x, axis, [(i, i ^ mask) for i in range(size)])


def local_call(kernel, name, outs, *args, hbm=(), scratch=(), mib=24, flops=10**9):
    return pl.pallas_call(
        kernel,
        out_shape=outs,
        in_specs=[HBM if i in hbm else VMEM for i in range(len(args))],
        out_specs=jax.tree.map(lambda _: VMEM, outs),
        scratch_shapes=scratch,
        name=name,
        compiler_params=params(mib),
        cost_estimate=pl.CostEstimate(flops=flops, bytes_accessed=1, transcendentals=0),
    )(*args)


def fetched(*args):
    return tuple(pltpu.VMEM(x.shape, x.dtype) for x in args) + (
        pltpu.SemaphoreType.DMA((len(args),)),
    )


def after(x, other):
    return lax.optimization_barrier((x, other))[0]


def per_device(queries, kv_pages, page_tables, lengths, owners, up_values, out_proj, residual,
               verify_states, norm_gain, route_ids, route_weights, expert_up):
    rows, _, key_width = queries.shape
    verify_rows, width = residual.shape
    n_expert, n_dp = lax.axis_size("expert"), lax.axis_size("dp")
    experts = n_expert * n_dp
    hidden = expert_up.shape[2]
    far = n_expert // NEAR
    far_groups = [[f * NEAR + n for f in range(far)] for n in range(NEAR)]
    shape = jax.ShapeDtypeStruct

    operands = (
        queries.reshape(rows, key_width),
        kv_pages.reshape(-1, key_width),
        page_tables.T,
        lengths.reshape(1, rows),
        owners.reshape(1, rows),
        up_values[0],
        out_proj[0],
    )
    partial_sums = local_call(
        functools.partial(attention_kernel, verify_rows),
        "attention",
        shape((far, NEAR * verify_rows, width), BF),
        *operands,
        hbm=range(7),
        scratch=fetched(*operands),
        mib=60,
        flops=4 * 10**9,
    )
    parts = lax.all_to_all(
        partial_sums, "expert", split_axis=0, concat_axis=0, tiled=True,
        axis_index_groups=far_groups,
    )
    near_sum = local_call(
        far_sum_kernel, "far_sum", shape((NEAR * verify_rows, width), BF), parts, residual
    )
    tokens = local_call(
        norm_draft_kernel,
        "norm_draft",
        shape((far, NEAR * verify_rows, width), BF),
        near_sum,
        swap(near_sum, "expert", n_expert, 1),
        after(norm_gain, partial_sums).reshape(1, width),
    )
    draft = lax.all_to_all(
        tokens, "expert", split_axis=0, concat_axis=0, tiled=True, axis_index_groups=far_groups
    )

    masks = [n_expert // 2] + [1 << i for i in range(n_expert.bit_length() - 2)]
    gathered, codes = verify_states.reshape(-1, width), [0]
    other = swap(verify_states, "expert", n_expert, masks[0]).reshape(-1, width)
    for step, mask in enumerate(masks):
        if step:
            gathered = after(gathered, partial_sums if step < len(masks) - 1 else near_sum)
            other = swap(gathered, "expert", n_expert, mask)
        gathered = jnp.concatenate([gathered, other], axis=0)
        codes += [code ^ (mask * n_dp) for code in codes]
    gathered_other = swap(after(gathered, tokens), "dp", n_dp, 1)
    codes += [code ^ 1 for code in codes]
    token_rows = experts * verify_rows * VERIFY
    active = local_call(
        functools.partial(expert_kernel, codes),
        "expert",
        shape((experts, VERIFY, verify_rows, hidden), BF),
        draft, swap(draft, "dp", n_dp, 1), gathered, gathered_other,
        after(norm_gain, partial_sums).reshape(1, width), expert_up[0],
        hbm=(5,),
        scratch=(
            pltpu.VMEM((width, hidden), BF),
            pltpu.VMEM((token_rows, width), BF),
            pltpu.SemaphoreType.DMA((CHUNKS,)),
        ),
        mib=52,
        flops=4 * 10**9,
    )
    back = lax.all_to_all(active, ("expert", "dp"), split_axis=0, concat_axis=0, tiled=True)
    return local_call(
        select_kernel,
        "select",
        shape((verify_rows, VERIFY, route_ids.shape[2], hidden), BF),
        route_ids.transpose(1, 0, 2), route_weights.transpose(1, 0, 2), back,
    )


def solution(mesh):
    placed = (
        P(("groups", "dp"), "expert", None),
        P(("groups", "dp"), None, None),
        P(("groups", "dp"), None),
        P(("groups", "dp")),
        P(("groups", "dp")),
        P("expert", None, None),
        P("expert", None, None),
        P(("groups", "expert", "dp"), None),
        P(("groups", "expert", "dp"), None, None),
        P(),
        P(("groups", "expert", "dp"), None, None),
        P(("groups", "expert", "dp"), None, None),
        P(("expert", "dp"), None, None),
    )
    return jax.shard_map(
        per_device,
        mesh=mesh,
        in_specs=placed,
        out_specs=P(("groups", "expert", "dp"), None, None, None),
        check_vma=False,
    )
```

time: 79.6 us -> 59.2 us (0.74)
  local copies, waits for them, and re-layouts: 12 us -> 0.12 us
  waiting for transfers between devices: 24.1 us -> 19 us
  starting transfers between devices: 16.7 us -> 13.4 us
  Pallas kernels: 7.62 us -> 10.7 us
  blocking collectives: 18.2 us -> 15.5 us
    unnamed x28 -> x11, local copies, waits for them, and re-layouts: 11.3 us -> 0.03 us
    all_to_all x1, waiting for transfers between devices: 0.01 us -> 7.8 us  [per_device(): lax.all_to_all(partial_sums, 'expert', split_axis=0, concat_axis=0, tiled...]
    all_to_all x1, waiting for transfers between devices: 13.2 us -> 6.36 us  [per_device(): lax.all_to_all(tokens, 'expert', split_axis=0, concat_axis=0, tiled=True,...]
    ppermute x4 -> x6, waiting for transfers between devices: 11 us -> 4.85 us  [swap(): return lax.ppermute(x, axis, [(i, i ^ mask) for i in range(size)])]
    pallas_call x5, Pallas kernels: 7.62 us -> 10.7 us  [local_call(): pl.pallas_call(kernel, out_shape=outs, in_specs=[HBM if i in hbm else VME...]
    all_to_all x1, blocking collectives: 18.2 us -> 15.5 us  [per_device(): lax.all_to_all(active, ('expert', 'dp'), split_axis=0, concat_axis=0, til...]
    all_to_all x1, starting transfers between devices: 5.5 us -> 3.38 us  [per_device(): lax.all_to_all(tokens, 'expert', split_axis=0, concat_axis=0, tiled=True,...]
    ppermute x4 -> x6, starting transfers between devices: 7.47 us -> 6.54 us  [swap(): return lax.ppermute(x, axis, [(i, i ^ mask) for i in range(size)])]
  transfers between devices with their start and end apart: 6 -> 8, of which waited for: 3 -> 4; matrix products, arithmetic and copies ran while one was open for 0% -> 0% of each run, Pallas kernels for 5% -> 9%
where the time goes in v2:
time: 59.2 us; the launch traced here: 58.9 us
  waiting for transfers between devices  19 us (32%)
  blocking collectives  15.5 us (26%)
  starting transfers between devices  13.4 us (23%)
  Pallas kernels  10.7 us (18%)
    all_to_all x1, blocking collectives, per_device(): lax.all_to_all(active, ('expert', 'dp'), split_axis=0, concat_axis=0, til...  15.5 us
    pallas_call x5, Pallas kernels, local_call(): pl.pallas_call(kernel, out_shape=outs, in_specs=[HBM if i in hbm else VME...  10.7 us
    all_to_all x1, waiting for transfers between devices, per_device(): lax.all_to_all(partial_sums, 'expert', split_axis=0, concat_axis=0, tiled...  7.8 us
    ppermute x6, starting transfers between devices, swap(): return lax.ppermute(x, axis, [(i, i ^ mask) for i in range(size)])  6.54 us
    all_to_all x1, waiting for transfers between devices, per_device(): lax.all_to_all(tokens, 'expert', split_axis=0, concat_axis=0, tiled=True,...  6.36 us
    ppermute x6, waiting for transfers between devices, swap(): return lax.ppermute(x, axis, [(i, i ^ mask) for i in range(size)])  4.85 us
    all_to_all x1, starting transfers between devices, per_device(): lax.all_to_all(partial_sums, 'expert', split_axis=0, concat_axis=0, tiled...  3.51 us
    all_to_all x1, starting transfers between devices, per_device(): lax.all_to_all(tokens, 'expert', split_axis=0, concat_axis=0, tiled=True,...  3.38 us
  transfers between devices with their start and end apart: 8, of which 4 were waited for; matrix products, arithmetic and copies ran while one was open for 0% of the time, Pallas kernels for 9%

profile of v2, /device:TPU:0, one launch (start us, length us, event | category | flops | bytes accessed | tf_op | source)
XLA Modules:
  0.0 58.9 jit_solution(8997229308371916120)
XLA Ops:
  0.0 4.0 %collective-permute-start.2 = (bf16[4,2,3584]{2,1,0:T(2,128)(2,1)}, bf16[4,2,3584]{2,1,0:T(2,128)(2,1)S(1)}, u32[]{:S(2)}, u32[]{:S(2)}) collective-permute-start(bf16[4,2,3584]{2,1,0:T(2,128)(2,1)} %param.21), channel_id=1, source_target_pairs={{0,8},{2,10},{4,12},{6,14},{8,0},{10,2},{12,4},{14,6},{1,9},{3,11}... | collective-permute-start | bytes 172040 | tf_op jit(solution)/shard_map/ppermute | solution.py:181
  4.0 4.6 %attention.1 = bf16[4,8,3584]{2,1,0:T(8,128)(2,1)} custom-call(bf16[32,576]{1,0:T(8,128)(2,1)} %bitcast.16, bf16[2048,576]{1,0:T(8,128)(2,1)} %bitcast.13, s32[8,32]{1,0:T(8,128)} %bitcast.17, s32[1,32]{1,0:T(1,128)} %bitcast.18, s32[1,32]{1,0:T(1,128)} %bitcast.19, bf16[512,128]{1,0:T(8,128)(2,1)} %bitcast.15, bf16[128,3584]{1,0:T(8,128)(2,1)} %bitcast.14), custom_call_target="tpu_custom_call" | custom-call | flops 4000000000 | bytes 1 | tf_op jit(solution)/shard_map/attention/pallas_call | solution.py:185
  8.7 0.0 collective-permute-done.2
  8.7 1.6 %collective-permute-start.3 = (bf16[16,3584]{1,0:T(8,128)(2,1)S(1)}, bf16[16,3584]{1,0:T(8,128)(2,1)S(1)}, u32[]{:S(2)}, u32[]{:S(2)}) collective-permute-start(bf16[16,3584]{1,0:T(8,128)(2,1)S(1)} %pad_maximum_fusion.1), channel_id=1, source_target_pairs={{0,2},{2,0},{4,6},{6,4},{8,10},{10,8},{12,14},{14,12},{1,3},{3,1},... | collective-permute-start | bytes 344072 | tf_op jit(solution)/shard_map/ppermute | solution.py:181
  10.3 3.5 %all-to-all-start = ((bf16[4,8,3584]{2,1,0:T(8,128)(2,1)}), bf16[4,8,3584]{2,1,0:T(8,128)(2,1)S(1)}, u32[]{:S(2)}, u32[]{:S(2)}) async-start(bf16[4,8,3584]{2,1,0:T(8,128)(2,1)} %attention.1), calls=%async_computation | async-start | bytes 458752 | tf_op jit(solution)/shard_map/all_to_all | solution.py:237
  13.8 0.0 copy-done.4
  13.8 0.0 collective-permute-done.3
  13.9 7.8 %all-to-all-done.parts_ref = bf16[4,8,3584]{2,1,0:T(8,128)(2,1)S(1)} async-done(((bf16[4,8,3584]{2,1,0:T(8,128)(2,1)}), bf16[4,8,3584]{2,1,0:T(8,128)(2,1)S(1)}, u32[]{:S(2)}, u32[]{:S(2)}) %all-to-all-start) | async-done | bytes 229408 | tf_op jit(solution)/shard_map/all_to_all | solution.py:237
  21.7 0.0 copy-done
  21.7 0.1 far_sum.1.mine_ref
  21.7 0.5 collective-permute-start
  22.2 0.4 collective-permute-start.4
  22.6 3.4 %collective-permute-done.theirs_ref = bf16[8,3584]{1,0:T(8,128)(2,1)S(1)} collective-permute-done((bf16[8,3584]{1,0:T(8,128)(2,1)S(1)}, bf16[8,3584]{1,0:T(8,128)(2,1)S(1)}, u32[]{:S(2)}, u32[]{:S(2)}) %collective-permute-start) | collective-permute-done | bytes 57376 | tf_op jit(solution)/shard_map/ppermute | solution.py:181
  26.0 0.8 %norm_draft.1 = bf16[4,8,3584]{2,1,0:T(8,128)(2,1)} custom-call(bf16[8,3584]{1,0:T(8,128)(2,1)S(1)} %far_sum.1.mine_ref, bf16[8,3584]{1,0:T(8,128)(2,1)S(1)} %collective-permute-done.theirs_ref, bf16[1,3584]{1,0:T(2,128)(2,1)S(1)} %reshape.26.gain_ref), custom_call_target="tpu_custom_call" | custom-call | flops 1000000000 | bytes 1 | tf_op jit(solution)/shard_map/norm_draft/pallas_call | solution.py:185
  26.8 3.4 %all-to-all-start.1 = ((bf16[4,8,3584]{2,1,0:T(8,128)(2,1)}), bf16[4,8,3584]{2,1,0:T(8,128)(2,1)S(1)}, u32[]{:S(2)}, u32[]{:S(2)}) async-start(bf16[4,8,3584]{2,1,0:T(8,128)(2,1)} %norm_draft.1), calls=%async_computation.1 | async-start | bytes 458752 | tf_op jit(solution)/shard_map/all_to_all | solution.py:252
  30.2 0.0 collective-permute-done.4
  30.2 0.1 collective-permute-start.5
  30.3 6.4 %all-to-all-done.1.draft_ref = bf16[4,8,3584]{2,1,0:T(8,128)(2,1)S(1)} async-done(((bf16[4,8,3584]{2,1,0:T(8,128)(2,1)}), bf16[4,8,3584]{2,1,0:T(8,128)(2,1)S(1)}, u32[]{:S(2)}, u32[]{:S(2)}) %all-to-all-start.1) | async-done | bytes 229408 | tf_op jit(solution)/shard_map/all_to_all | solution.py:252
  36.7 0.0 collective-permute-start.1
  36.7 1.5 %collective-permute-done.1.draft_other_ref = bf16[4,8,3584]{2,1,0:T(8,128)(2,1)S(1)} collective-permute-done((bf16[4,8,3584]{2,1,0:T(8,128)(2,1)S(1)}, bf16[4,8,3584]{2,1,0:T(8,128)(2,1)S(1)}, u32[]{:S(2)}, u32[]{:S(2)}) %collective-permute-start.1) | collective-permute-done | bytes 229408 | tf_op jit(solution)/shard_map/ppermute | solution.py:181
  38.1 0.0 collective-permute-done.5.verify_other_ref
  38.1 3.6 %expert.1 = bf16[16,3,4,1024]{3,2,1,0:T(4,128)(2,1)S(1)} custom-call(bf16[4,8,3584]{2,1,0:T(8,128)(2,1)S(1)} %all-to-all-done.1.draft_ref, bf16[4,8,3584]{2,1,0:T(8,128)(2,1)S(1)} %collective-permute-done.1.draft_other_ref, bf16[64,3584]{1,0:T(8,128)(2,1)S(1)} %constant_dynamic-update-slice_fusion.verify_ref, ...), custom_call_target="tpu_custom_call" | custom-call | flops 4000000000 | bytes 1 | tf_op jit(solution)/shard_map/expert/pallas_call | solution.py:185
  41.8 15.5 %all_to_all.15.back_ref = bf16[16,3,4,1024]{3,2,1,0:T(4,128)(2,1)S(1)} all-to-all(bf16[16,3,4,1024]{3,2,1,0:T(4,128)(2,1)S(1)} %expert.1), channel_id=1, replica_groups=mesh['groups'=2,'expert'=8,'dp'=2] {'expert','dp'}, dimensions={0} | all-to-all | bytes 786432 | tf_op jit(solution)/shard_map/all_to_all | solution.py:283
  57.3 1.6 %select.1 = bf16[4,3,8,1024]{3,2,1,0:T(8,128)(2,1)} custom-call(s32[3,4,8]{2,1,0:T(4,128)S(1)} %bitcast.10, f32[3,4,8]{2,1,0:T(4,128)S(1)} %bitcast.11, bf16[16,3,4,1024]{3,2,1,0:T(4,128)(2,1)S(1)} %all_to_all.15.back_ref), custom_call_target="tpu_custom_call" | custom-call | flops 1000000000 | bytes 1 | tf_op jit(solution)/shard_map/select/pallas_call | solution.py:185
  (15 shorter events, 0.1 us)
Async XLA Ops:
  0.0 8.7 %collective-permute-start.2 = (bf16[4,2,3584]{2,1,0:T(2,128)(2,1)}, bf16[4,2,3584]{2,1,0:T(2,128)(2,1)S(1)}, u32[]{:S(2)}, u32[]{:S(2)}) collective-permute-start(bf16[4,2,3584]{2,1,0:T(2,128)(2,1)} %param.21), channel_id=1, source_target_pairs={{0,8},{2,10},{4,12},{6,14},{8,0},{10,2},{12,4},{14,6},{1,9},{3,11}... | collective-permute-start | bytes 172040 | tf_op jit(solution)/shard_map/ppermute | solution.py:181
  4.0 4.6 %copy-start.3 = (bf16[4,2,3584]{2,1,0:T(2,128)(2,1)S(1)}, bf16[4,2,3584]{2,1,0:T(2,128)(2,1)}, u32[]{:S(2)}) copy-start(bf16[4,2,3584]{2,1,0:T(2,128)(2,1)} %param.21) | copy-start | bytes 172036
  4.0 9.8 %copy-start.4 = (bf16[3584]{0:T(1024)(128)(2,1)S(1)}, bf16[3584]{0:T(1024)(128)(2,1)}, u32[]{:S(2)}) copy-start(bf16[3584]{0:T(1024)(128)(2,1)} %param.22) | copy-start | bytes 21508
  4.0 17.6 %copy-start = (bf16[4,3584]{1,0:T(4,128)(2,1)S(1)}, bf16[4,3584]{1,0:T(4,128)(2,1)}, u32[]{:S(2)}) copy-start(bf16[4,3584]{1,0:T(4,128)(2,1)} %residual_ref.1) | copy-start | bytes 86020
  8.7 5.1 %collective-permute-start.3 = (bf16[16,3584]{1,0:T(8,128)(2,1)S(1)}, bf16[16,3584]{1,0:T(8,128)(2,1)S(1)}, u32[]{:S(2)}, u32[]{:S(2)}) collective-permute-start(bf16[16,3584]{1,0:T(8,128)(2,1)S(1)} %pad_maximum_fusion.1), channel_id=1, source_target_pairs={{0,2},{2,0},{4,6},{6,4},{8,10},{10,8},{12,14},{14,12},{1,3},{3,1},... | collective-permute-start | bytes 344072 | tf_op jit(solution)/shard_map/ppermute | solution.py:181
  10.3 11.4 %all-to-all-start = ((bf16[4,8,3584]{2,1,0:T(8,128)(2,1)}), bf16[4,8,3584]{2,1,0:T(8,128)(2,1)S(1)}, u32[]{:S(2)}, u32[]{:S(2)}) async-start(bf16[4,8,3584]{2,1,0:T(8,128)(2,1)} %attention.1), calls=%async_computation | async-start | bytes 458752 | tf_op jit(solution)/shard_map/all_to_all | solution.py:237
  21.7 4.2 %collective-permute-start = (bf16[8,3584]{1,0:T(8,128)(2,1)S(1)}, bf16[8,3584]{1,0:T(8,128)(2,1)S(1)}, u32[]{:S(2)}, u32[]{:S(2)}) collective-permute-start(bf16[8,3584]{1,0:T(8,128)(2,1)S(1)} %far_sum.1.mine_ref), channel_id=1, source_target_pairs={{0,2},{2,0},{4,6},{6,4},{8,10},{10,8},{12,14},{14,12},{1,3},{3,1},... | collective-permute-start | bytes 172040 | tf_op jit(solution)/shard_map/ppermute | solution.py:181
  22.2 8.0 %collective-permute-start.4 = (bf16[32,3584]{1,0:T(8,128)(2,1)S(1)}, bf16[32,3584]{1,0:T(8,128)(2,1)S(1)}, u32[]{:S(2)}, u32[]{:S(2)}) collective-permute-start(bf16[32,3584]{1,0:T(8,128)(2,1)S(1)} %pad_maximum_fusion), channel_id=1, source_target_pairs={{0,4},{2,6},{4,0},{6,2},{8,12},{10,14},{12,8},{14,10},{1,5},{3,7},... | collective-permute-start | bytes 688136 | tf_op jit(solution)/shard_map/ppermute | solution.py:181
  26.8 9.9 %all-to-all-start.1 = ((bf16[4,8,3584]{2,1,0:T(8,128)(2,1)}), bf16[4,8,3584]{2,1,0:T(8,128)(2,1)S(1)}, u32[]{:S(2)}, u32[]{:S(2)}) async-start(bf16[4,8,3584]{2,1,0:T(8,128)(2,1)} %norm_draft.1), calls=%async_computation.1 | async-start | bytes 458752 | tf_op jit(solution)/shard_map/all_to_all | solution.py:252
  30.2 7.9 %collective-permute-start.5 = (bf16[64,3584]{1,0:T(8,128)(2,1)S(1)}, bf16[64,3584]{1,0:T(8,128)(2,1)S(1)}, u32[]{:S(2)}, u32[]{:S(2)}) collective-permute-start(bf16[64,3584]{1,0:T(8,128)(2,1)S(1)} %constant_dynamic-update-slice_fusion.verify_ref), channel_id=1, source_target_pairs={{0,1},{1,0},{2,3},{3,2},{4,5},{5,4},{6,7},{7,6},{8,9},{9,8},{10,11... | collective-permute-start | bytes 1376264 | tf_op jit(solution)/shard_map/ppermute | solution.py:181
  36.7 1.5 %collective-permute-start.1 = (bf16[4,8,3584]{2,1,0:T(8,128)(2,1)S(1)}, bf16[4,8,3584]{2,1,0:T(8,128)(2,1)S(1)}, u32[]{:S(2)}, u32[]{:S(2)}) collective-permute-start(bf16[4,8,3584]{2,1,0:T(8,128)(2,1)S(1)} %all-to-all-done.1.draft_ref), channel_id=1, source_target_pairs={{0,1},{1,0},{2,3},{3,2},{4,5},{5,4},{6,7},{7,6},{8,9},{9,8},{10,11... | collective-permute-start | bytes 688136 | tf_op jit(solution)/shard_map/ppermute | solution.py:181
  38.1 19.1 %copy-start.1 = (s32[4,3,8]{2,0,1:T(4,128)S(1)}, s32[4,3,8]{2,0,1:T(4,128)}, u32[]{:S(2)}) copy-start(s32[4,3,8]{2,0,1:T(4,128)} %param.23) | copy-start | bytes 1156
  38.1 19.1 %copy-start.2 = (f32[4,3,8]{2,0,1:T(4,128)S(1)}, f32[4,3,8]{2,0,1:T(4,128)}, u32[]{:S(2)}) copy-start(f32[4,3,8]{2,0,1:T(4,128)} %param.24) | copy-start | bytes 1156

commit v3 on v2

--- a/solution.py
+++ b/solution.py
@@ -14,6 +14,7 @@
 PAGES = 32
 NEAR = 2
 CHUNKS = 7
+KV_CHUNKS = 4
 ROW_BLOCK = 256
 BF = jnp.bfloat16
 F32 = jnp.float32
@@ -44,8 +45,18 @@
 
 def attention_kernel(per_owner, *refs):
     sources, sum_ref, targets, semaphores = refs[:7], refs[7], refs[8:15], refs[15]
-    copies = fetch(sources, targets, semaphores)
-    q_ref, kv_ref, table_ref, length_ref, owner_ref, up_ref, out_ref = targets
+    table_ref, length_ref, owner_ref, q_ref, up_ref, out_ref, kv_ref = targets
+    small = fetch(sources[:4], targets[:4], semaphores)
+    part = kv_ref.shape[0] // KV_CHUNKS
+    chunks = [
+        pltpu.make_async_copy(
+            sources[6].at[pl.ds(i * part, part)], kv_ref.at[pl.ds(i * part, part)], semaphores.at[6 + i]
+        )
+        for i in range(KV_CHUNKS)
+    ]
+    for copy in chunks:
+        copy.start()
+    weights = fetch(sources[4:6], targets[4:6], semaphores.at[pl.ds(4, 2)])
     rows = q_ref.shape[0]
     tokens = kv_ref.shape[0]
     slots = table_ref.shape[0]
@@ -53,7 +64,7 @@
     token = lax.broadcasted_iota(jnp.int32, (1, tokens), 1)
     page, offset = token // page_len, token % page_len
     position = jnp.full((rows, tokens), 1 << 24, jnp.int32)
-    for copy in copies[2:5]:
+    for copy in small:
         copy.wait()
     for slot in range(slots):
         named = as_column(table_ref[slot : slot + 1, :], rows)
@@ -64,17 +75,24 @@
     second = lax.broadcasted_iota(jnp.int32, (rows, rows), 1)
     before = (as_column(owner, rows) == owner) & (first < second)
     target = owner * per_owner + jnp.sum(before.astype(jnp.int32), axis=0, keepdims=True)
-    for copy in copies[:2]:
+    scores = []
+    for i, copy in enumerate(chunks):
         copy.wait()
-    scores = lax.dot_general(
-        q_ref[...], kv_ref[...], (((1,), (1,)), ((), ())), preferred_element_type=F32
-    ) * (VHEAD + ROPE) ** (-0.5)
+        scores.append(
+            lax.dot_general(
+                q_ref[...],
+                kv_ref[i * part : (i + 1) * part],
+                (((1,), (1,)), ((), ())),
+                preferred_element_type=F32,
+            )
+        )
+    scores = jnp.concatenate(scores, axis=1) * (VHEAD + ROPE) ** (-0.5)
     masked = jnp.where(visible, scores, -1e30)
     row_max = jnp.max(masked, axis=1, keepdims=True)
     exponent = jnp.where(visible, jnp.exp(masked - row_max), 0.0)
     attention = (exponent / jnp.sum(exponent, axis=1, keepdims=True)).astype(BF)
     context = jnp.dot(attention, kv_ref[:, :LATENT], preferred_element_type=F32).astype(BF)
-    for copy in copies[5:]:
+    for copy in weights:
         copy.wait()
     values = jnp.dot(context, up_ref[...], preferred_element_type=F32).astype(BF)
     picked = jnp.dot((first == target).astype(BF), values, preferred_element_type=F32).astype(BF)
@@ -158,23 +176,32 @@
 
 
 def select_kernel(ids_ref, gates_ref, back_ref, out_ref):
-    devices, _, per, _ = back_ref.shape
+    devices, groups, per, width = back_ref.shape
     top = ids_ref.shape[2]
     eye = lax.broadcasted_iota(jnp.int32, (top, top), 0) == lax.broadcasted_iota(
         jnp.int32, (top, top), 1
     )
-    source = lax.broadcasted_iota(jnp.int32, (top, devices), 1)
-    for t in range(ids_ref.shape[0]):
-        for q in range(ids_ref.shape[1]):
+    source = lax.broadcasted_iota(jnp.int32, (top, devices * per), 1)
+    for group in range(groups):
+        places, chosen, gates = [], [], []
+        for r in range(per):
+            if group == 0:
+                q, t = r, 0
+            else:
+                q, t = divmod((group - 1) * per + r, VERIFY - 1)
+                t += 1
             ids = jnp.sum(jnp.where(eye, ids_ref[t, q : q + 1, :], 0), axis=1, keepdims=True)
-            gates = jnp.sum(
-                jnp.where(eye, gates_ref[t, q : q + 1, :], 0.0), axis=1, keepdims=True
+            gates.append(
+                jnp.sum(jnp.where(eye, gates_ref[t, q : q + 1, :], 0.0), axis=1, keepdims=True)
             )
-            chosen = (ids == source).astype(BF)
-            place = q if t == 0 else per + q * (VERIFY - 1) + t - 1
-            rows = back_ref[:, place // per, place % per, :]
-            active = jnp.dot(chosen, rows, preferred_element_type=F32)
-            out_ref[q, t] = (gates * active).astype(BF)
+            chosen.append((ids * per + r == source).astype(F32))
+            places.append((q, t))
+        rows = back_ref[:, group].reshape(devices * per, width)
+        active = jnp.dot(
+            jnp.concatenate(chosen, axis=0).astype(BF), rows, preferred_element_type=F32
+        )
+        for r, (q, t) in enumerate(places):
+            out_ref[q, t] = (gates[r] * active[r * top : (r + 1) * top]).astype(BF)
 
 
 def swap(x, axis, size, mask):
@@ -194,9 +221,9 @@
     )(*args)
 
 
-def fetched(*args):
+def fetched(*args, more=0):
     return tuple(pltpu.VMEM(x.shape, x.dtype) for x in args) + (
-        pltpu.SemaphoreType.DMA((len(args),)),
+        pltpu.SemaphoreType.DMA((len(args) + more,)),
     )
 
 
@@ -216,13 +243,13 @@
     shape = jax.ShapeDtypeStruct
 
     operands = (
-        queries.reshape(rows, key_width),
-        kv_pages.reshape(-1, key_width),
         page_tables.T,
         lengths.reshape(1, rows),
         owners.reshape(1, rows),
+        queries.reshape(rows, key_width),
         up_values[0],
         out_proj[0],
+        kv_pages.reshape(-1, key_width),
     )
     partial_sums = local_call(
         functools.partial(attention_kernel, verify_rows),
@@ -230,16 +257,16 @@
         shape((far, NEAR * verify_rows, width), BF),
         *operands,
         hbm=range(7),
-        scratch=fetched(*operands),
+        scratch=fetched(*operands, more=KV_CHUNKS - 1),
         mib=60,
-        flops=4 * 10**9,
+        flops=4000000000,
     )
     parts = lax.all_to_all(
         partial_sums, "expert", split_axis=0, concat_axis=0, tiled=True,
         axis_index_groups=far_groups,
     )
     near_sum = local_call(
-        far_sum_kernel, "far_sum", shape((NEAR * verify_rows, width), BF), parts, residual
+        far_sum_kernel, "far_sum", shape((NEAR * verify_rows, width), BF), parts, residual, flops=1000000000,
     )
     tokens = local_call(
         norm_draft_kernel,
@@ -258,11 +285,16 @@
     other = swap(verify_states, "expert", n_expert, masks[0]).reshape(-1, width)
     for step, mask in enumerate(masks):
         if step:
-            gathered = after(gathered, partial_sums if step < len(masks) - 1 else near_sum)
             other = swap(gathered, "expert", n_expert, mask)
+        if step < len(masks) - 2:
+            gathered = gathered
+        elif step < len(masks) - 1:
+            gathered = after(gathered, near_sum)
+        else:
+            gathered = after(gathered, tokens)
         gathered = jnp.concatenate([gathered, other], axis=0)
         codes += [code ^ (mask * n_dp) for code in codes]
-    gathered_other = swap(after(gathered, tokens), "dp", n_dp, 1)
+    gathered_other = swap(gathered, "dp", n_dp, 1)
     codes += [code ^ 1 for code in codes]
     token_rows = experts * verify_rows * VERIFY
     active = local_call(

time: 59.2 us -> 57.7 us (0.975)
  waiting for transfers between devices: 19 us -> 16.5 us
  starting transfers between devices: 13.4 us -> 14.4 us
  Pallas kernels: 10.7 us -> 9.76 us
  blocking collectives: 15.5 us -> 16.4 us
    all_to_all x1, waiting for transfers between devices: 7.8 us -> 6.48 us  [per_device(): lax.all_to_all(partial_sums, 'expert', split_axis=0, concat_axis=0, tiled...]
    ppermute x6, waiting for transfers between devices: 4.85 us -> 3.73 us  [swap(): return lax.ppermute(x, axis, [(i, i ^ mask) for i in range(size)])]
    ppermute x6, starting transfers between devices: 6.54 us -> 7.63 us  [swap(): return lax.ppermute(x, axis, [(i, i ^ mask) for i in range(size)])]
    pallas_call x5, Pallas kernels: 10.7 us -> 9.76 us  [local_call(): pl.pallas_call(kernel, out_shape=outs, in_specs=[HBM if i in hbm else VME...]
    all_to_all x1, blocking collectives: 15.5 us -> 16.4 us  [per_device(): lax.all_to_all(active, ('expert', 'dp'), split_axis=0, concat_axis=0, til...]
where the time goes in v3:
time: 57.7 us; the launch traced here: 57.4 us
  waiting for transfers between devices  16.5 us (29%)
  blocking collectives  16.4 us (28%)
  starting transfers between devices  14.4 us (25%)
  Pallas kernels  9.76 us (17%)
    all_to_all x1, blocking collectives, per_device(): lax.all_to_all(active, ('expert', 'dp'), split_axis=0, concat_axis=0, til...  16.4 us
    pallas_call x5, Pallas kernels, local_call(): pl.pallas_call(kernel, out_shape=outs, in_specs=[HBM if i in hbm else VME...  9.76 us
    ppermute x6, starting transfers between devices, swap(): return lax.ppermute(x, axis, [(i, i ^ mask) for i in range(size)])  7.63 us
    all_to_all x1, waiting for transfers between devices, per_device(): lax.all_to_all(partial_sums, 'expert', split_axis=0, concat_axis=0, tiled...  6.48 us
    all_to_all x1, waiting for transfers between devices, per_device(): lax.all_to_all(tokens, 'expert', split_axis=0, concat_axis=0, tiled=True,...  6.34 us
    ppermute x6, waiting for transfers between devices, swap(): return lax.ppermute(x, axis, [(i, i ^ mask) for i in range(size)])  3.73 us
    all_to_all x1, starting transfers between devices, per_device(): lax.all_to_all(partial_sums, 'expert', split_axis=0, concat_axis=0, tiled...  3.4 us
    all_to_all x1, starting transfers between devices, per_device(): lax.all_to_all(tokens, 'expert', split_axis=0, concat_axis=0, tiled=True,...  3.38 us
  transfers between devices with their start and end apart: 8, of which 4 were waited for; matrix products, arithmetic and copies ran while one was open for 0% of the time, Pallas kernels for 9%

profile of v3, /device:TPU:0, one launch (start us, length us, event | category | flops | bytes accessed | tf_op | source)
XLA Modules:
  0.0 57.4 jit_solution(2564250951425644557)
XLA Ops:
  0.0 4.0 %collective-permute-start.2 = (bf16[4,2,3584]{2,1,0:T(2,128)(2,1)}, bf16[4,2,3584]{2,1,0:T(2,128)(2,1)S(1)}, u32[]{:S(2)}, u32[]{:S(2)}) collective-permute-start(bf16[4,2,3584]{2,1,0:T(2,128)(2,1)} %param.21), channel_id=1, source_target_pairs={{0,8},{2,10},{4,12},{6,14},{8,0},{10,2},{12,4},{14,6},{1,9},{3,11}... | collective-permute-start | bytes 172040 | tf_op jit(solution)/shard_map/ppermute | solution.py:208
  4.0 4.3 %attention.1 = bf16[4,8,3584]{2,1,0:T(8,128)(2,1)} custom-call(s32[8,32]{1,0:T(8,128)} %bitcast.17, s32[1,32]{1,0:T(1,128)} %bitcast.18, s32[1,32]{1,0:T(1,128)} %bitcast.19, bf16[32,576]{1,0:T(8,128)(2,1)} %bitcast.16, bf16[512,128]{1,0:T(8,128)(2,1)} %bitcast.15, bf16[128,3584]{1,0:T(8,128)(2,1)} %bitcast.14, bf16[2048,576]{1,0:T(8,128)(2,1)} %bitcast.13), custom_call_target="tpu_custom_call" | custom-call | flops 4000000000 | bytes 1 | tf_op jit(solution)/shard_map/attention/pallas_call | solution.py:212
  8.3 3.4 %all-to-all-start = ((bf16[4,8,3584]{2,1,0:T(8,128)(2,1)}), bf16[4,8,3584]{2,1,0:T(8,128)(2,1)S(1)}, u32[]{:S(2)}, u32[]{:S(2)}) async-start(bf16[4,8,3584]{2,1,0:T(8,128)(2,1)} %attention.1), calls=%async_computation | async-start | bytes 458752 | tf_op jit(solution)/shard_map/all_to_all | solution.py:264
  11.7 0.0 copy-done.3
  11.8 0.0 collective-permute-done.2
  11.9 1.6 %collective-permute-start.3 = (bf16[16,3584]{1,0:T(8,128)(2,1)S(1)}, bf16[16,3584]{1,0:T(8,128)(2,1)S(1)}, u32[]{:S(2)}, u32[]{:S(2)}) collective-permute-start(bf16[16,3584]{1,0:T(8,128)(2,1)S(1)} %constant_dynamic-update-slice_fusion), channel_id=1, source_target_pairs={{0,2},{2,0},{4,6},{6,4},{8,10},{10,8},{12,14},{14,12},{1,3},{3,1},... | collective-permute-start | bytes 344072 | tf_op jit(solution)/shard_map/ppermute | solution.py:208
  13.4 6.5 %all-to-all-done.parts_ref = bf16[4,8,3584]{2,1,0:T(8,128)(2,1)S(1)} async-done(((bf16[4,8,3584]{2,1,0:T(8,128)(2,1)}), bf16[4,8,3584]{2,1,0:T(8,128)(2,1)S(1)}, u32[]{:S(2)}, u32[]{:S(2)}) %all-to-all-start) | async-done | bytes 229408 | tf_op jit(solution)/shard_map/all_to_all | solution.py:264
  19.9 0.1 far_sum.1.mine_ref
  20.0 1.6 %collective-permute-start = (bf16[8,3584]{1,0:T(8,128)(2,1)S(1)}, bf16[8,3584]{1,0:T(8,128)(2,1)S(1)}, u32[]{:S(2)}, u32[]{:S(2)}) collective-permute-start(bf16[8,3584]{1,0:T(8,128)(2,1)S(1)} %far_sum.1.mine_ref), channel_id=1, source_target_pairs={{0,2},{2,0},{4,6},{6,4},{8,10},{10,8},{12,14},{14,12},{1,3},{3,1},... | collective-permute-start | bytes 172040 | tf_op jit(solution)/shard_map/ppermute | solution.py:208
  21.5 0.0 collective-permute-done.3
  21.6 0.4 collective-permute-start.4
  22.0 2.2 %collective-permute-done.theirs_ref = bf16[8,3584]{1,0:T(8,128)(2,1)S(1)} collective-permute-done((bf16[8,3584]{1,0:T(8,128)(2,1)S(1)}, bf16[8,3584]{1,0:T(8,128)(2,1)S(1)}, u32[]{:S(2)}, u32[]{:S(2)}) %collective-permute-start) | collective-permute-done | bytes 57376 | tf_op jit(solution)/shard_map/ppermute | solution.py:208
  24.2 0.8 %norm_draft.1 = bf16[4,8,3584]{2,1,0:T(8,128)(2,1)} custom-call(bf16[8,3584]{1,0:T(8,128)(2,1)S(1)} %far_sum.1.mine_ref, bf16[8,3584]{1,0:T(8,128)(2,1)S(1)} %collective-permute-done.theirs_ref, bf16[1,3584]{1,0:T(2,128)(2,1)S(1)} %reshape.26.gain_ref), custom_call_target="tpu_custom_call" | custom-call | flops 1000000000 | bytes 1 | tf_op jit(solution)/shard_map/norm_draft/pallas_call | solution.py:212
  25.0 3.4 %all-to-all-start.1 = ((bf16[4,8,3584]{2,1,0:T(8,128)(2,1)}), bf16[4,8,3584]{2,1,0:T(8,128)(2,1)S(1)}, u32[]{:S(2)}, u32[]{:S(2)}) async-start(bf16[4,8,3584]{2,1,0:T(8,128)(2,1)} %norm_draft.1), calls=%async_computation.1 | async-start | bytes 458752 | tf_op jit(solution)/shard_map/all_to_all | solution.py:279
  28.5 0.0 collective-permute-done.4
  28.5 0.1 collective-permute-start.5
  28.6 6.3 %all-to-all-done.1.draft_ref = bf16[4,8,3584]{2,1,0:T(8,128)(2,1)S(1)} async-done(((bf16[4,8,3584]{2,1,0:T(8,128)(2,1)}), bf16[4,8,3584]{2,1,0:T(8,128)(2,1)S(1)}, u32[]{:S(2)}, u32[]{:S(2)}) %all-to-all-start.1) | async-done | bytes 229408 | tf_op jit(solution)/shard_map/all_to_all | solution.py:279
  34.9 0.0 collective-permute-start.1
  34.9 1.5 %collective-permute-done.1.draft_other_ref = bf16[4,8,3584]{2,1,0:T(8,128)(2,1)S(1)} collective-permute-done((bf16[4,8,3584]{2,1,0:T(8,128)(2,1)S(1)}, bf16[4,8,3584]{2,1,0:T(8,128)(2,1)S(1)}, u32[]{:S(2)}, u32[]{:S(2)}) %collective-permute-start.1) | collective-permute-done | bytes 229408 | tf_op jit(solution)/shard_map/ppermute | solution.py:208
  36.4 0.0 collective-permute-done.5.verify_other_ref
  36.4 3.6 %expert.1 = bf16[16,3,4,1024]{3,2,1,0:T(4,128)(2,1)S(1)} custom-call(bf16[4,8,3584]{2,1,0:T(8,128)(2,1)S(1)} %all-to-all-done.1.draft_ref, bf16[4,8,3584]{2,1,0:T(8,128)(2,1)S(1)} %collective-permute-done.1.draft_other_ref, bf16[64,3584]{1,0:T(8,128)(2,1)S(1)} %constant_dynamic-update-slice_fusion.4.verify_ref, ...), custom_call_target="tpu_custom_call" | custom-call | flops 4000000000 | bytes 1 | tf_op jit(solution)/shard_map/expert/pallas_call | solution.py:212
  40.1 16.4 %all_to_all.15.back_ref = bf16[16,3,4,1024]{3,2,1,0:T(4,128)(2,1)S(1)} all-to-all(bf16[16,3,4,1024]{3,2,1,0:T(4,128)(2,1)S(1)} %expert.1), channel_id=1, replica_groups=mesh['groups'=2,'expert'=8,'dp'=2] {'expert','dp'}, dimensions={0} | all-to-all | bytes 786432 | tf_op jit(solution)/shard_map/all_to_all | solution.py:315
  56.5 0.0 copy-done.1
  56.5 0.9 %select.1 = bf16[4,3,8,1024]{3,2,1,0:T(8,128)(2,1)} custom-call(s32[3,4,8]{2,1,0:T(4,128)S(1)} %bitcast.10, f32[3,4,8]{2,1,0:T(4,128)S(1)} %bitcast.11, bf16[16,3,4,1024]{3,2,1,0:T(4,128)(2,1)S(1)} %all_to_all.15.back_ref), custom_call_target="tpu_custom_call" | custom-call | flops 1000000000 | bytes 1 | tf_op jit(solution)/shard_map/select/pallas_call | solution.py:212
  (17 shorter events, 0.1 us)
Async XLA Ops:
  0.0 11.8 %collective-permute-start.2 = (bf16[4,2,3584]{2,1,0:T(2,128)(2,1)}, bf16[4,2,3584]{2,1,0:T(2,128)(2,1)S(1)}, u32[]{:S(2)}, u32[]{:S(2)}) collective-permute-start(bf16[4,2,3584]{2,1,0:T(2,128)(2,1)} %param.21), channel_id=1, source_target_pairs={{0,8},{2,10},{4,12},{6,14},{8,0},{10,2},{12,4},{14,6},{1,9},{3,11}... | collective-permute-start | bytes 172040 | tf_op jit(solution)/shard_map/ppermute | solution.py:208
  4.0 7.7 %copy-start.3 = (bf16[4,2,3584]{2,1,0:T(2,128)(2,1)S(1)}, bf16[4,2,3584]{2,1,0:T(2,128)(2,1)}, u32[]{:S(2)}) copy-start(bf16[4,2,3584]{2,1,0:T(2,128)(2,1)} %param.21) | copy-start | bytes 172036
  4.0 7.8 %copy-start.4 = (bf16[3584]{0:T(1024)(128)(2,1)S(1)}, bf16[3584]{0:T(1024)(128)(2,1)}, u32[]{:S(2)}) copy-start(bf16[3584]{0:T(1024)(128)(2,1)} %param.22) | copy-start | bytes 21508
  4.0 15.9 %copy-start = (bf16[4,3584]{1,0:T(4,128)(2,1)S(1)}, bf16[4,3584]{1,0:T(4,128)(2,1)}, u32[]{:S(2)}) copy-start(bf16[4,3584]{1,0:T(4,128)(2,1)} %residual_ref.1) | copy-start | bytes 86020
  8.3 11.6 %all-to-all-start = ((bf16[4,8,3584]{2,1,0:T(8,128)(2,1)}), bf16[4,8,3584]{2,1,0:T(8,128)(2,1)S(1)}, u32[]{:S(2)}, u32[]{:S(2)}) async-start(bf16[4,8,3584]{2,1,0:T(8,128)(2,1)} %attention.1), calls=%async_computation | async-start | bytes 458752 | tf_op jit(solution)/shard_map/all_to_all | solution.py:264
  11.9 9.7 %collective-permute-start.3 = (bf16[16,3584]{1,0:T(8,128)(2,1)S(1)}, bf16[16,3584]{1,0:T(8,128)(2,1)S(1)}, u32[]{:S(2)}, u32[]{:S(2)}) collective-permute-start(bf16[16,3584]{1,0:T(8,128)(2,1)S(1)} %constant_dynamic-update-slice_fusion), channel_id=1, source_target_pairs={{0,2},{2,0},{4,6},{6,4},{8,10},{10,8},{12,14},{14,12},{1,3},{3,1},... | collective-permute-start | bytes 344072 | tf_op jit(solution)/shard_map/ppermute | solution.py:208
  20.0 4.2 %collective-permute-start = (bf16[8,3584]{1,0:T(8,128)(2,1)S(1)}, bf16[8,3584]{1,0:T(8,128)(2,1)S(1)}, u32[]{:S(2)}, u32[]{:S(2)}) collective-permute-start(bf16[8,3584]{1,0:T(8,128)(2,1)S(1)} %far_sum.1.mine_ref), channel_id=1, source_target_pairs={{0,2},{2,0},{4,6},{6,4},{8,10},{10,8},{12,14},{14,12},{1,3},{3,1},... | collective-permute-start | bytes 172040 | tf_op jit(solution)/shard_map/ppermute | solution.py:208
  21.6 6.9 %collective-permute-start.4 = (bf16[32,3584]{1,0:T(8,128)(2,1)S(1)}, bf16[32,3584]{1,0:T(8,128)(2,1)S(1)}, u32[]{:S(2)}, u32[]{:S(2)}) collective-permute-start(bf16[32,3584]{1,0:T(8,128)(2,1)S(1)} %constant_dynamic-update-slice_fusion.2), channel_id=1, source_target_pairs={{0,4},{2,6},{4,0},{6,2},{8,12},{10,14},{12,8},{14,10},{1,5},{3,7},... | collective-permute-start | bytes 688136 | tf_op jit(solution)/shard_map/ppermute | solution.py:208
  25.0 9.9 %all-to-all-start.1 = ((bf16[4,8,3584]{2,1,0:T(8,128)(2,1)}), bf16[4,8,3584]{2,1,0:T(8,128)(2,1)S(1)}, u32[]{:S(2)}, u32[]{:S(2)}) async-start(bf16[4,8,3584]{2,1,0:T(8,128)(2,1)} %norm_draft.1), calls=%async_computation.1 | async-start | bytes 458752 | tf_op jit(solution)/shard_map/all_to_all | solution.py:279
  28.5 7.9 %collective-permute-start.5 = (bf16[64,3584]{1,0:T(8,128)(2,1)S(1)}, bf16[64,3584]{1,0:T(8,128)(2,1)S(1)}, u32[]{:S(2)}, u32[]{:S(2)}) collective-permute-start(bf16[64,3584]{1,0:T(8,128)(2,1)S(1)} %constant_dynamic-update-slice_fusion.4.verify_ref), channel_id=1, source_target_pairs={{0,1},{1,0},{2,3},{3,2},{4,5},{5,4},{6,7},{7,6},{8,9},{9,8},{10,11... | collective-permute-start | bytes 1376264 | tf_op jit(solution)/shard_map/ppermute | solution.py:208
  34.9 1.5 %collective-permute-start.1 = (bf16[4,8,3584]{2,1,0:T(8,128)(2,1)S(1)}, bf16[4,8,3584]{2,1,0:T(8,128)(2,1)S(1)}, u32[]{:S(2)}, u32[]{:S(2)}) collective-permute-start(bf16[4,8,3584]{2,1,0:T(8,128)(2,1)S(1)} %all-to-all-done.1.draft_ref), channel_id=1, source_target_pairs={{0,1},{1,0},{2,3},{3,2},{4,5},{5,4},{6,7},{7,6},{8,9},{9,8},{10,11... | collective-permute-start | bytes 688136 | tf_op jit(solution)/shard_map/ppermute | solution.py:208
  36.4 20.0 %copy-start.1 = (s32[4,3,8]{2,0,1:T(4,128)S(1)}, s32[4,3,8]{2,0,1:T(4,128)}, u32[]{:S(2)}) copy-start(s32[4,3,8]{2,0,1:T(4,128)} %param.23) | copy-start | bytes 1156
  36.4 20.1 %copy-start.2 = (f32[4,3,8]{2,0,1:T(4,128)S(1)}, f32[4,3,8]{2,0,1:T(4,128)}, u32[]{:S(2)}) copy-start(f32[4,3,8]{2,0,1:T(4,128)} %param.24) | copy-start | bytes 1156

commit v4 on v3

--- a/solution.py
+++ b/solution.py
@@ -13,8 +13,8 @@
 VERIFY = 3
 PAGES = 32
 NEAR = 2
-CHUNKS = 7
-KV_CHUNKS = 4
+CHUNKS = 4
+KV_CHUNKS = 2
 ROW_BLOCK = 256
 BF = jnp.bfloat16
 F32 = jnp.float32

time: 57.7 us -> 58.3 us (1.010)
  no operation moved by 1% of the time
where the time goes in v4:
time: 58.3 us; the launch traced here: 58 us
  waiting for transfers between devices  16.6 us (28%)
  blocking collectives  16.4 us (28%)
  starting transfers between devices  14.4 us (25%)
  Pallas kernels  10.3 us (18%)
    all_to_all x1, blocking collectives, per_device(): lax.all_to_all(active, ('expert', 'dp'), split_axis=0, concat_axis=0, til...  16.4 us
    pallas_call x5, Pallas kernels, local_call(): pl.pallas_call(kernel, out_shape=outs, in_specs=[HBM if i in hbm else VME...  10.3 us
    ppermute x6, starting transfers between devices, swap(): return lax.ppermute(x, axis, [(i, i ^ mask) for i in range(size)])  7.63 us
    all_to_all x1, waiting for transfers between devices, per_device(): lax.all_to_all(partial_sums, 'expert', split_axis=0, concat_axis=0, tiled...  6.48 us
    all_to_all x1, waiting for transfers between devices, per_device(): lax.all_to_all(tokens, 'expert', split_axis=0, concat_axis=0, tiled=True,...  6.34 us
    ppermute x6, waiting for transfers between devices, swap(): return lax.ppermute(x, axis, [(i, i ^ mask) for i in range(size)])  3.74 us
    all_to_all x1, starting transfers between devices, per_device(): lax.all_to_all(partial_sums, 'expert', split_axis=0, concat_axis=0, tiled...  3.4 us
    all_to_all x1, starting transfers between devices, per_device(): lax.all_to_all(tokens, 'expert', split_axis=0, concat_axis=0, tiled=True,...  3.38 us
  transfers between devices with their start and end apart: 8, of which 4 were waited for; matrix products, arithmetic and copies ran while one was open for 0% of the time, Pallas kernels for 9%

profile of v4, /device:TPU:0, one launch (start us, length us, event | category | flops | bytes accessed | tf_op | source)
XLA Modules:
  0.0 58.0 jit_solution(2096583968546512923)
XLA Ops:
  0.0 4.0 %collective-permute-start.2 = (bf16[4,2,3584]{2,1,0:T(2,128)(2,1)}, bf16[4,2,3584]{2,1,0:T(2,128)(2,1)S(1)}, u32[]{:S(2)}, u32[]{:S(2)}) collective-permute-start(bf16[4,2,3584]{2,1,0:T(2,128)(2,1)} %param.21), channel_id=1, source_target_pairs={{0,8},{2,10},{4,12},{6,14},{8,0},{10,2},{12,4},{14,6},{1,9},{3,11}... | collective-permute-start | bytes 172040 | tf_op jit(solution)/shard_map/ppermute | solution.py:208
  4.0 4.3 %attention.1 = bf16[4,8,3584]{2,1,0:T(8,128)(2,1)} custom-call(s32[8,32]{1,0:T(8,128)} %bitcast.17, s32[1,32]{1,0:T(1,128)} %bitcast.18, s32[1,32]{1,0:T(1,128)} %bitcast.19, bf16[32,576]{1,0:T(8,128)(2,1)} %bitcast.16, bf16[512,128]{1,0:T(8,128)(2,1)} %bitcast.15, bf16[128,3584]{1,0:T(8,128)(2,1)} %bitcast.14, bf16[2048,576]{1,0:T(8,128)(2,1)} %bitcast.13), custom_call_target="tpu_custom_call" | custom-call | flops 4000000000 | bytes 1 | tf_op jit(solution)/shard_map/attention/pallas_call | solution.py:212
  8.3 3.4 %all-to-all-start = ((bf16[4,8,3584]{2,1,0:T(8,128)(2,1)}), bf16[4,8,3584]{2,1,0:T(8,128)(2,1)S(1)}, u32[]{:S(2)}, u32[]{:S(2)}) async-start(bf16[4,8,3584]{2,1,0:T(8,128)(2,1)} %attention.1), calls=%async_computation | async-start | bytes 458752 | tf_op jit(solution)/shard_map/all_to_all | solution.py:264
  11.7 0.0 copy-done.3
  11.8 0.0 copy-done.4
  11.8 0.0 collective-permute-done.2
  11.9 1.6 %collective-permute-start.3 = (bf16[16,3584]{1,0:T(8,128)(2,1)S(1)}, bf16[16,3584]{1,0:T(8,128)(2,1)S(1)}, u32[]{:S(2)}, u32[]{:S(2)}) collective-permute-start(bf16[16,3584]{1,0:T(8,128)(2,1)S(1)} %constant_dynamic-update-slice_fusion), channel_id=1, source_target_pairs={{0,2},{2,0},{4,6},{6,4},{8,10},{10,8},{12,14},{14,12},{1,3},{3,1},... | collective-permute-start | bytes 344072 | tf_op jit(solution)/shard_map/ppermute | solution.py:208
  13.4 6.5 %all-to-all-done.parts_ref = bf16[4,8,3584]{2,1,0:T(8,128)(2,1)S(1)} async-done(((bf16[4,8,3584]{2,1,0:T(8,128)(2,1)}), bf16[4,8,3584]{2,1,0:T(8,128)(2,1)S(1)}, u32[]{:S(2)}, u32[]{:S(2)}) %all-to-all-start) | async-done | bytes 229408 | tf_op jit(solution)/shard_map/all_to_all | solution.py:264
  19.9 0.1 far_sum.1.mine_ref
  20.0 1.6 %collective-permute-start = (bf16[8,3584]{1,0:T(8,128)(2,1)S(1)}, bf16[8,3584]{1,0:T(8,128)(2,1)S(1)}, u32[]{:S(2)}, u32[]{:S(2)}) collective-permute-start(bf16[8,3584]{1,0:T(8,128)(2,1)S(1)} %far_sum.1.mine_ref), channel_id=1, source_target_pairs={{0,2},{2,0},{4,6},{6,4},{8,10},{10,8},{12,14},{14,12},{1,3},{3,1},... | collective-permute-start | bytes 172040 | tf_op jit(solution)/shard_map/ppermute | solution.py:208
  21.5 0.0 collective-permute-done.3
  21.6 0.4 collective-permute-start.4
  22.0 2.2 %collective-permute-done.theirs_ref = bf16[8,3584]{1,0:T(8,128)(2,1)S(1)} collective-permute-done((bf16[8,3584]{1,0:T(8,128)(2,1)S(1)}, bf16[8,3584]{1,0:T(8,128)(2,1)S(1)}, u32[]{:S(2)}, u32[]{:S(2)}) %collective-permute-start) | collective-permute-done | bytes 57376 | tf_op jit(solution)/shard_map/ppermute | solution.py:208
  24.2 0.8 %norm_draft.1 = bf16[4,8,3584]{2,1,0:T(8,128)(2,1)} custom-call(bf16[8,3584]{1,0:T(8,128)(2,1)S(1)} %far_sum.1.mine_ref, bf16[8,3584]{1,0:T(8,128)(2,1)S(1)} %collective-permute-done.theirs_ref, bf16[1,3584]{1,0:T(2,128)(2,1)S(1)} %reshape.26.gain_ref), custom_call_target="tpu_custom_call" | custom-call | flops 1000000000 | bytes 1 | tf_op jit(solution)/shard_map/norm_draft/pallas_call | solution.py:212
  25.0 3.4 %all-to-all-start.1 = ((bf16[4,8,3584]{2,1,0:T(8,128)(2,1)}), bf16[4,8,3584]{2,1,0:T(8,128)(2,1)S(1)}, u32[]{:S(2)}, u32[]{:S(2)}) async-start(bf16[4,8,3584]{2,1,0:T(8,128)(2,1)} %norm_draft.1), calls=%async_computation.1 | async-start | bytes 458752 | tf_op jit(solution)/shard_map/all_to_all | solution.py:279
  28.4 0.0 collective-permute-done.4
  28.5 0.1 collective-permute-start.5
  28.6 6.3 %all-to-all-done.1.draft_ref = bf16[4,8,3584]{2,1,0:T(8,128)(2,1)S(1)} async-done(((bf16[4,8,3584]{2,1,0:T(8,128)(2,1)}), bf16[4,8,3584]{2,1,0:T(8,128)(2,1)S(1)}, u32[]{:S(2)}, u32[]{:S(2)}) %all-to-all-start.1) | async-done | bytes 229408 | tf_op jit(solution)/shard_map/all_to_all | solution.py:279
  34.9 0.0 collective-permute-start.1
  34.9 1.5 %collective-permute-done.1.draft_other_ref = bf16[4,8,3584]{2,1,0:T(8,128)(2,1)S(1)} collective-permute-done((bf16[4,8,3584]{2,1,0:T(8,128)(2,1)S(1)}, bf16[4,8,3584]{2,1,0:T(8,128)(2,1)S(1)}, u32[]{:S(2)}, u32[]{:S(2)}) %collective-permute-start.1) | collective-permute-done | bytes 229408 | tf_op jit(solution)/shard_map/ppermute | solution.py:208
  36.4 0.0 collective-permute-done.5.verify_other_ref
  36.4 4.2 %expert.1 = bf16[16,3,4,1024]{3,2,1,0:T(4,128)(2,1)S(1)} custom-call(bf16[4,8,3584]{2,1,0:T(8,128)(2,1)S(1)} %all-to-all-done.1.draft_ref, bf16[4,8,3584]{2,1,0:T(8,128)(2,1)S(1)} %collective-permute-done.1.draft_other_ref, bf16[64,3584]{1,0:T(8,128)(2,1)S(1)} %constant_dynamic-update-slice_fusion.4.verify_ref, ...), custom_call_target="tpu_custom_call" | custom-call | flops 4000000000 | bytes 1 | tf_op jit(solution)/shard_map/expert/pallas_call | solution.py:212
  40.6 16.4 %all_to_all.15.back_ref = bf16[16,3,4,1024]{3,2,1,0:T(4,128)(2,1)S(1)} all-to-all(bf16[16,3,4,1024]{3,2,1,0:T(4,128)(2,1)S(1)} %expert.1), channel_id=1, replica_groups=mesh['groups'=2,'expert'=8,'dp'=2] {'expert','dp'}, dimensions={0} | all-to-all | bytes 786432 | tf_op jit(solution)/shard_map/all_to_all | solution.py:315
  57.0 0.9 %select.1 = bf16[4,3,8,1024]{3,2,1,0:T(8,128)(2,1)} custom-call(s32[3,4,8]{2,1,0:T(4,128)S(1)} %bitcast.10, f32[3,4,8]{2,1,0:T(4,128)S(1)} %bitcast.11, bf16[16,3,4,1024]{3,2,1,0:T(4,128)(2,1)S(1)} %all_to_all.15.back_ref), custom_call_target="tpu_custom_call" | custom-call | flops 1000000000 | bytes 1 | tf_op jit(solution)/shard_map/select/pallas_call | solution.py:212
  (17 shorter events, 0.1 us)
Async XLA Ops:
  0.0 11.8 %collective-permute-start.2 = (bf16[4,2,3584]{2,1,0:T(2,128)(2,1)}, bf16[4,2,3584]{2,1,0:T(2,128)(2,1)S(1)}, u32[]{:S(2)}, u32[]{:S(2)}) collective-permute-start(bf16[4,2,3584]{2,1,0:T(2,128)(2,1)} %param.21), channel_id=1, source_target_pairs={{0,8},{2,10},{4,12},{6,14},{8,0},{10,2},{12,4},{14,6},{1,9},{3,11}... | collective-permute-start | bytes 172040 | tf_op jit(solution)/shard_map/ppermute | solution.py:208
  4.0 7.7 %copy-start.3 = (bf16[4,2,3584]{2,1,0:T(2,128)(2,1)S(1)}, bf16[4,2,3584]{2,1,0:T(2,128)(2,1)}, u32[]{:S(2)}) copy-start(bf16[4,2,3584]{2,1,0:T(2,128)(2,1)} %param.21) | copy-start | bytes 172036
  4.0 7.7 %copy-start.4 = (bf16[3584]{0:T(1024)(128)(2,1)S(1)}, bf16[3584]{0:T(1024)(128)(2,1)}, u32[]{:S(2)}) copy-start(bf16[3584]{0:T(1024)(128)(2,1)} %param.22) | copy-start | bytes 21508
  4.0 15.9 %copy-start = (bf16[4,3584]{1,0:T(4,128)(2,1)S(1)}, bf16[4,3584]{1,0:T(4,128)(2,1)}, u32[]{:S(2)}) copy-start(bf16[4,3584]{1,0:T(4,128)(2,1)} %residual_ref.1) | copy-start | bytes 86020
  8.3 11.6 %all-to-all-start = ((bf16[4,8,3584]{2,1,0:T(8,128)(2,1)}), bf16[4,8,3584]{2,1,0:T(8,128)(2,1)S(1)}, u32[]{:S(2)}, u32[]{:S(2)}) async-start(bf16[4,8,3584]{2,1,0:T(8,128)(2,1)} %attention.1), calls=%async_computation | async-start | bytes 458752 | tf_op jit(solution)/shard_map/all_to_all | solution.py:264
  11.9 9.7 %collective-permute-start.3 = (bf16[16,3584]{1,0:T(8,128)(2,1)S(1)}, bf16[16,3584]{1,0:T(8,128)(2,1)S(1)}, u32[]{:S(2)}, u32[]{:S(2)}) collective-permute-start(bf16[16,3584]{1,0:T(8,128)(2,1)S(1)} %constant_dynamic-update-slice_fusion), channel_id=1, source_target_pairs={{0,2},{2,0},{4,6},{6,4},{8,10},{10,8},{12,14},{14,12},{1,3},{3,1},... | collective-permute-start | bytes 344072 | tf_op jit(solution)/shard_map/ppermute | solution.py:208
  20.0 4.2 %collective-permute-start = (bf16[8,3584]{1,0:T(8,128)(2,1)S(1)}, bf16[8,3584]{1,0:T(8,128)(2,1)S(1)}, u32[]{:S(2)}, u32[]{:S(2)}) collective-permute-start(bf16[8,3584]{1,0:T(8,128)(2,1)S(1)} %far_sum.1.mine_ref), channel_id=1, source_target_pairs={{0,2},{2,0},{4,6},{6,4},{8,10},{10,8},{12,14},{14,12},{1,3},{3,1},... | collective-permute-start | bytes 172040 | tf_op jit(solution)/shard_map/ppermute | solution.py:208
  21.6 6.9 %collective-permute-start.4 = (bf16[32,3584]{1,0:T(8,128)(2,1)S(1)}, bf16[32,3584]{1,0:T(8,128)(2,1)S(1)}, u32[]{:S(2)}, u32[]{:S(2)}) collective-permute-start(bf16[32,3584]{1,0:T(8,128)(2,1)S(1)} %constant_dynamic-update-slice_fusion.2), channel_id=1, source_target_pairs={{0,4},{2,6},{4,0},{6,2},{8,12},{10,14},{12,8},{14,10},{1,5},{3,7},... | collective-permute-start | bytes 688136 | tf_op jit(solution)/shard_map/ppermute | solution.py:208
  25.0 9.9 %all-to-all-start.1 = ((bf16[4,8,3584]{2,1,0:T(8,128)(2,1)}), bf16[4,8,3584]{2,1,0:T(8,128)(2,1)S(1)}, u32[]{:S(2)}, u32[]{:S(2)}) async-start(bf16[4,8,3584]{2,1,0:T(8,128)(2,1)} %norm_draft.1), calls=%async_computation.1 | async-start | bytes 458752 | tf_op jit(solution)/shard_map/all_to_all | solution.py:279
  28.5 7.9 %collective-permute-start.5 = (bf16[64,3584]{1,0:T(8,128)(2,1)S(1)}, bf16[64,3584]{1,0:T(8,128)(2,1)S(1)}, u32[]{:S(2)}, u32[]{:S(2)}) collective-permute-start(bf16[64,3584]{1,0:T(8,128)(2,1)S(1)} %constant_dynamic-update-slice_fusion.4.verify_ref), channel_id=1, source_target_pairs={{0,1},{1,0},{2,3},{3,2},{4,5},{5,4},{6,7},{7,6},{8,9},{9,8},{10,11... | collective-permute-start | bytes 1376264 | tf_op jit(solution)/shard_map/ppermute | solution.py:208
  34.9 1.5 %collective-permute-start.1 = (bf16[4,8,3584]{2,1,0:T(8,128)(2,1)S(1)}, bf16[4,8,3584]{2,1,0:T(8,128)(2,1)S(1)}, u32[]{:S(2)}, u32[]{:S(2)}) collective-permute-start(bf16[4,8,3584]{2,1,0:T(8,128)(2,1)S(1)} %all-to-all-done.1.draft_ref), channel_id=1, source_target_pairs={{0,1},{1,0},{2,3},{3,2},{4,5},{5,4},{6,7},{7,6},{8,9},{9,8},{10,11... | collective-permute-start | bytes 688136 | tf_op jit(solution)/shard_map/ppermute | solution.py:208
  36.4 20.6 %copy-start.1 = (s32[4,3,8]{2,0,1:T(4,128)S(1)}, s32[4,3,8]{2,0,1:T(4,128)}, u32[]{:S(2)}) copy-start(s32[4,3,8]{2,0,1:T(4,128)} %param.23) | copy-start | bytes 1156
  36.4 20.6 %copy-start.2 = (f32[4,3,8]{2,0,1:T(4,128)S(1)}, f32[4,3,8]{2,0,1:T(4,128)}, u32[]{:S(2)}) copy-start(f32[4,3,8]{2,0,1:T(4,128)} %param.24) | copy-start | bytes 1156

commit v5 on v4

--- a/solution.py
+++ b/solution.py
@@ -13,7 +13,7 @@
 VERIFY = 3
 PAGES = 32
 NEAR = 2
-CHUNKS = 4
+CHUNKS = 7
 KV_CHUNKS = 2
 ROW_BLOCK = 256
 BF = jnp.bfloat16

time: 58.3 us -> 57.7 us (0.990)
  no operation moved by 1% of the time
where the time goes in v5:
time: 57.7 us; the launch traced here: 57.4 us
  waiting for transfers between devices  16.6 us (29%)
  blocking collectives  16.4 us (28%)
  starting transfers between devices  14.4 us (25%)
  Pallas kernels  9.75 us (17%)
    all_to_all x1, blocking collectives, per_device(): lax.all_to_all(active, ('expert', 'dp'), split_axis=0, concat_axis=0, til...  16.4 us
    pallas_call x5, Pallas kernels, local_call(): pl.pallas_call(kernel, out_shape=outs, in_specs=[HBM if i in hbm else VME...  9.75 us
    ppermute x6, starting transfers between devices, swap(): return lax.ppermute(x, axis, [(i, i ^ mask) for i in range(size)])  7.63 us
    all_to_all x1, waiting for transfers between devices, per_device(): lax.all_to_all(partial_sums, 'expert', split_axis=0, concat_axis=0, tiled...  6.48 us
    all_to_all x1, waiting for transfers between devices, per_device(): lax.all_to_all(tokens, 'expert', split_axis=0, concat_axis=0, tiled=True,...  6.34 us
    ppermute x6, waiting for transfers between devices, swap(): return lax.ppermute(x, axis, [(i, i ^ mask) for i in range(size)])  3.74 us
    all_to_all x1, starting transfers between devices, per_device(): lax.all_to_all(partial_sums, 'expert', split_axis=0, concat_axis=0, tiled...  3.4 us
    all_to_all x1, starting transfers between devices, per_device(): lax.all_to_all(tokens, 'expert', split_axis=0, concat_axis=0, tiled=True,...  3.38 us
  transfers between devices with their start and end apart: 8, of which 4 were waited for; matrix products, arithmetic and copies ran while one was open for 0% of the time, Pallas kernels for 9%

profile of v5, /device:TPU:0, one launch (start us, length us, event | category | flops | bytes accessed | tf_op | source)
XLA Modules:
  0.0 57.4 jit_solution(3991713317101796496)
XLA Ops:
  0.0 4.0 %collective-permute-start.2 = (bf16[4,2,3584]{2,1,0:T(2,128)(2,1)}, bf16[4,2,3584]{2,1,0:T(2,128)(2,1)S(1)}, u32[]{:S(2)}, u32[]{:S(2)}) collective-permute-start(bf16[4,2,3584]{2,1,0:T(2,128)(2,1)} %param.21), channel_id=1, source_target_pairs={{0,8},{2,10},{4,12},{6,14},{8,0},{10,2},{12,4},{14,6},{1,9},{3,11}... | collective-permute-start | bytes 172040 | tf_op jit(solution)/shard_map/ppermute | solution.py:208
  4.0 4.3 %attention.1 = bf16[4,8,3584]{2,1,0:T(8,128)(2,1)} custom-call(s32[8,32]{1,0:T(8,128)} %bitcast.17, s32[1,32]{1,0:T(1,128)} %bitcast.18, s32[1,32]{1,0:T(1,128)} %bitcast.19, bf16[32,576]{1,0:T(8,128)(2,1)} %bitcast.16, bf16[512,128]{1,0:T(8,128)(2,1)} %bitcast.15, bf16[128,3584]{1,0:T(8,128)(2,1)} %bitcast.14, bf16[2048,576]{1,0:T(8,128)(2,1)} %bitcast.13), custom_call_target="tpu_custom_call" | custom-call | flops 4000000000 | bytes 1 | tf_op jit(solution)/shard_map/attention/pallas_call | solution.py:212
  8.3 3.4 %all-to-all-start = ((bf16[4,8,3584]{2,1,0:T(8,128)(2,1)}), bf16[4,8,3584]{2,1,0:T(8,128)(2,1)S(1)}, u32[]{:S(2)}, u32[]{:S(2)}) async-start(bf16[4,8,3584]{2,1,0:T(8,128)(2,1)} %attention.1), calls=%async_computation | async-start | bytes 458752 | tf_op jit(solution)/shard_map/all_to_all | solution.py:264
  11.7 0.0 copy-done.3
  11.8 0.0 copy-done.4
  11.8 0.0 collective-permute-done.2
  11.9 1.6 %collective-permute-start.3 = (bf16[16,3584]{1,0:T(8,128)(2,1)S(1)}, bf16[16,3584]{1,0:T(8,128)(2,1)S(1)}, u32[]{:S(2)}, u32[]{:S(2)}) collective-permute-start(bf16[16,3584]{1,0:T(8,128)(2,1)S(1)} %constant_dynamic-update-slice_fusion), channel_id=1, source_target_pairs={{0,2},{2,0},{4,6},{6,4},{8,10},{10,8},{12,14},{14,12},{1,3},{3,1},... | collective-permute-start | bytes 344072 | tf_op jit(solution)/shard_map/ppermute | solution.py:208
  13.4 6.5 %all-to-all-done.parts_ref = bf16[4,8,3584]{2,1,0:T(8,128)(2,1)S(1)} async-done(((bf16[4,8,3584]{2,1,0:T(8,128)(2,1)}), bf16[4,8,3584]{2,1,0:T(8,128)(2,1)S(1)}, u32[]{:S(2)}, u32[]{:S(2)}) %all-to-all-start) | async-done | bytes 229408 | tf_op jit(solution)/shard_map/all_to_all | solution.py:264
  19.9 0.1 far_sum.1.mine_ref
  20.0 1.6 %collective-permute-start = (bf16[8,3584]{1,0:T(8,128)(2,1)S(1)}, bf16[8,3584]{1,0:T(8,128)(2,1)S(1)}, u32[]{:S(2)}, u32[]{:S(2)}) collective-permute-start(bf16[8,3584]{1,0:T(8,128)(2,1)S(1)} %far_sum.1.mine_ref), channel_id=1, source_target_pairs={{0,2},{2,0},{4,6},{6,4},{8,10},{10,8},{12,14},{14,12},{1,3},{3,1},... | collective-permute-start | bytes 172040 | tf_op jit(solution)/shard_map/ppermute | solution.py:208
  21.5 0.0 collective-permute-done.3
  21.6 0.4 collective-permute-start.4
  22.0 2.2 %collective-permute-done.theirs_ref = bf16[8,3584]{1,0:T(8,128)(2,1)S(1)} collective-permute-done((bf16[8,3584]{1,0:T(8,128)(2,1)S(1)}, bf16[8,3584]{1,0:T(8,128)(2,1)S(1)}, u32[]{:S(2)}, u32[]{:S(2)}) %collective-permute-start) | collective-permute-done | bytes 57376 | tf_op jit(solution)/shard_map/ppermute | solution.py:208
  24.2 0.8 %norm_draft.1 = bf16[4,8,3584]{2,1,0:T(8,128)(2,1)} custom-call(bf16[8,3584]{1,0:T(8,128)(2,1)S(1)} %far_sum.1.mine_ref, bf16[8,3584]{1,0:T(8,128)(2,1)S(1)} %collective-permute-done.theirs_ref, bf16[1,3584]{1,0:T(2,128)(2,1)S(1)} %reshape.26.gain_ref), custom_call_target="tpu_custom_call" | custom-call | flops 1000000000 | bytes 1 | tf_op jit(solution)/shard_map/norm_draft/pallas_call | solution.py:212
  25.0 3.4 %all-to-all-start.1 = ((bf16[4,8,3584]{2,1,0:T(8,128)(2,1)}), bf16[4,8,3584]{2,1,0:T(8,128)(2,1)S(1)}, u32[]{:S(2)}, u32[]{:S(2)}) async-start(bf16[4,8,3584]{2,1,0:T(8,128)(2,1)} %norm_draft.1), calls=%async_computation.1 | async-start | bytes 458752 | tf_op jit(solution)/shard_map/all_to_all | solution.py:279
  28.4 0.0 collective-permute-done.4
  28.5 0.1 collective-permute-start.5
  28.6 6.3 %all-to-all-done.1.draft_ref = bf16[4,8,3584]{2,1,0:T(8,128)(2,1)S(1)} async-done(((bf16[4,8,3584]{2,1,0:T(8,128)(2,1)}), bf16[4,8,3584]{2,1,0:T(8,128)(2,1)S(1)}, u32[]{:S(2)}, u32[]{:S(2)}) %all-to-all-start.1) | async-done | bytes 229408 | tf_op jit(solution)/shard_map/all_to_all | solution.py:279
  34.9 0.0 collective-permute-start.1
  34.9 1.5 %collective-permute-done.1.draft_other_ref = bf16[4,8,3584]{2,1,0:T(8,128)(2,1)S(1)} collective-permute-done((bf16[4,8,3584]{2,1,0:T(8,128)(2,1)S(1)}, bf16[4,8,3584]{2,1,0:T(8,128)(2,1)S(1)}, u32[]{:S(2)}, u32[]{:S(2)}) %collective-permute-start.1) | collective-permute-done | bytes 229408 | tf_op jit(solution)/shard_map/ppermute | solution.py:208
  36.4 0.0 collective-permute-done.5.verify_other_ref
  36.4 3.7 %expert.1 = bf16[16,3,4,1024]{3,2,1,0:T(4,128)(2,1)S(1)} custom-call(bf16[4,8,3584]{2,1,0:T(8,128)(2,1)S(1)} %all-to-all-done.1.draft_ref, bf16[4,8,3584]{2,1,0:T(8,128)(2,1)S(1)} %collective-permute-done.1.draft_other_ref, bf16[64,3584]{1,0:T(8,128)(2,1)S(1)} %constant_dynamic-update-slice_fusion.4.verify_ref, ...), custom_call_target="tpu_custom_call" | custom-call | flops 4000000000 | bytes 1 | tf_op jit(solution)/shard_map/expert/pallas_call | solution.py:212
  40.1 16.4 %all_to_all.15.back_ref = bf16[16,3,4,1024]{3,2,1,0:T(4,128)(2,1)S(1)} all-to-all(bf16[16,3,4,1024]{3,2,1,0:T(4,128)(2,1)S(1)} %expert.1), channel_id=1, replica_groups=mesh['groups'=2,'expert'=8,'dp'=2] {'expert','dp'}, dimensions={0} | all-to-all | bytes 786432 | tf_op jit(solution)/shard_map/all_to_all | solution.py:315
  56.4 0.9 %select.1 = bf16[4,3,8,1024]{3,2,1,0:T(8,128)(2,1)} custom-call(s32[3,4,8]{2,1,0:T(4,128)S(1)} %bitcast.10, f32[3,4,8]{2,1,0:T(4,128)S(1)} %bitcast.11, bf16[16,3,4,1024]{3,2,1,0:T(4,128)(2,1)S(1)} %all_to_all.15.back_ref), custom_call_target="tpu_custom_call" | custom-call | flops 1000000000 | bytes 1 | tf_op jit(solution)/shard_map/select/pallas_call | solution.py:212
  (17 shorter events, 0.1 us)
Async XLA Ops:
  0.0 11.8 %collective-permute-start.2 = (bf16[4,2,3584]{2,1,0:T(2,128)(2,1)}, bf16[4,2,3584]{2,1,0:T(2,128)(2,1)S(1)}, u32[]{:S(2)}, u32[]{:S(2)}) collective-permute-start(bf16[4,2,3584]{2,1,0:T(2,128)(2,1)} %param.21), channel_id=1, source_target_pairs={{0,8},{2,10},{4,12},{6,14},{8,0},{10,2},{12,4},{14,6},{1,9},{3,11}... | collective-permute-start | bytes 172040 | tf_op jit(solution)/shard_map/ppermute | solution.py:208
  4.0 7.7 %copy-start.3 = (bf16[4,2,3584]{2,1,0:T(2,128)(2,1)S(1)}, bf16[4,2,3584]{2,1,0:T(2,128)(2,1)}, u32[]{:S(2)}) copy-start(bf16[4,2,3584]{2,1,0:T(2,128)(2,1)} %param.21) | copy-start | bytes 172036
  4.0 7.7 %copy-start.4 = (bf16[3584]{0:T(1024)(128)(2,1)S(1)}, bf16[3584]{0:T(1024)(128)(2,1)}, u32[]{:S(2)}) copy-start(bf16[3584]{0:T(1024)(128)(2,1)} %param.22) | copy-start | bytes 21508
  4.0 15.9 %copy-start = (bf16[4,3584]{1,0:T(4,128)(2,1)S(1)}, bf16[4,3584]{1,0:T(4,128)(2,1)}, u32[]{:S(2)}) copy-start(bf16[4,3584]{1,0:T(4,128)(2,1)} %residual_ref.1) | copy-start | bytes 86020
  8.3 11.6 %all-to-all-start = ((bf16[4,8,3584]{2,1,0:T(8,128)(2,1)}), bf16[4,8,3584]{2,1,0:T(8,128)(2,1)S(1)}, u32[]{:S(2)}, u32[]{:S(2)}) async-start(bf16[4,8,3584]{2,1,0:T(8,128)(2,1)} %attention.1), calls=%async_computation | async-start | bytes 458752 | tf_op jit(solution)/shard_map/all_to_all | solution.py:264
  11.9 9.7 %collective-permute-start.3 = (bf16[16,3584]{1,0:T(8,128)(2,1)S(1)}, bf16[16,3584]{1,0:T(8,128)(2,1)S(1)}, u32[]{:S(2)}, u32[]{:S(2)}) collective-permute-start(bf16[16,3584]{1,0:T(8,128)(2,1)S(1)} %constant_dynamic-update-slice_fusion), channel_id=1, source_target_pairs={{0,2},{2,0},{4,6},{6,4},{8,10},{10,8},{12,14},{14,12},{1,3},{3,1},... | collective-permute-start | bytes 344072 | tf_op jit(solution)/shard_map/ppermute | solution.py:208
  20.0 4.2 %collective-permute-start = (bf16[8,3584]{1,0:T(8,128)(2,1)S(1)}, bf16[8,3584]{1,0:T(8,128)(2,1)S(1)}, u32[]{:S(2)}, u32[]{:S(2)}) collective-permute-start(bf16[8,3584]{1,0:T(8,128)(2,1)S(1)} %far_sum.1.mine_ref), channel_id=1, source_target_pairs={{0,2},{2,0},{4,6},{6,4},{8,10},{10,8},{12,14},{14,12},{1,3},{3,1},... | collective-permute-start | bytes 172040 | tf_op jit(solution)/shard_map/ppermute | solution.py:208
  21.6 6.9 %collective-permute-start.4 = (bf16[32,3584]{1,0:T(8,128)(2,1)S(1)}, bf16[32,3584]{1,0:T(8,128)(2,1)S(1)}, u32[]{:S(2)}, u32[]{:S(2)}) collective-permute-start(bf16[32,3584]{1,0:T(8,128)(2,1)S(1)} %constant_dynamic-update-slice_fusion.2), channel_id=1, source_target_pairs={{0,4},{2,6},{4,0},{6,2},{8,12},{10,14},{12,8},{14,10},{1,5},{3,7},... | collective-permute-start | bytes 688136 | tf_op jit(solution)/shard_map/ppermute | solution.py:208
  25.0 9.9 %all-to-all-start.1 = ((bf16[4,8,3584]{2,1,0:T(8,128)(2,1)}), bf16[4,8,3584]{2,1,0:T(8,128)(2,1)S(1)}, u32[]{:S(2)}, u32[]{:S(2)}) async-start(bf16[4,8,3584]{2,1,0:T(8,128)(2,1)} %norm_draft.1), calls=%async_computation.1 | async-start | bytes 458752 | tf_op jit(solution)/shard_map/all_to_all | solution.py:279
  28.5 7.9 %collective-permute-start.5 = (bf16[64,3584]{1,0:T(8,128)(2,1)S(1)}, bf16[64,3584]{1,0:T(8,128)(2,1)S(1)}, u32[]{:S(2)}, u32[]{:S(2)}) collective-permute-start(bf16[64,3584]{1,0:T(8,128)(2,1)S(1)} %constant_dynamic-update-slice_fusion.4.verify_ref), channel_id=1, source_target_pairs={{0,1},{1,0},{2,3},{3,2},{4,5},{5,4},{6,7},{7,6},{8,9},{9,8},{10,11... | collective-permute-start | bytes 1376264 | tf_op jit(solution)/shard_map/ppermute | solution.py:208
  34.9 1.5 %collective-permute-start.1 = (bf16[4,8,3584]{2,1,0:T(8,128)(2,1)S(1)}, bf16[4,8,3584]{2,1,0:T(8,128)(2,1)S(1)}, u32[]{:S(2)}, u32[]{:S(2)}) collective-permute-start(bf16[4,8,3584]{2,1,0:T(8,128)(2,1)S(1)} %all-to-all-done.1.draft_ref), channel_id=1, source_target_pairs={{0,1},{1,0},{2,3},{3,2},{4,5},{5,4},{6,7},{7,6},{8,9},{9,8},{10,11... | collective-permute-start | bytes 688136 | tf_op jit(solution)/shard_map/ppermute | solution.py:208
  36.4 20.0 %copy-start.1 = (s32[4,3,8]{2,0,1:T(4,128)S(1)}, s32[4,3,8]{2,0,1:T(4,128)}, u32[]{:S(2)}) copy-start(s32[4,3,8]{2,0,1:T(4,128)} %param.23) | copy-start | bytes 1156
  36.4 20.0 %copy-start.2 = (f32[4,3,8]{2,0,1:T(4,128)S(1)}, f32[4,3,8]{2,0,1:T(4,128)}, u32[]{:S(2)}) copy-start(f32[4,3,8]{2,0,1:T(4,128)} %param.24) | copy-start | bytes 1156

commit v6 on v5

--- a/solution.py
+++ b/solution.py
@@ -14,7 +14,7 @@
 PAGES = 32
 NEAR = 2
 CHUNKS = 7
-KV_CHUNKS = 2
+KV_CHUNKS = 1
 ROW_BLOCK = 256
 BF = jnp.bfloat16
 F32 = jnp.float32

time: 57.7 us -> 58 us (level)
  no operation moved by 1% of the time
where the time goes in v6:
time: 58 us; the launch traced here: 57.7 us
  waiting for transfers between devices  16.5 us (28%)
  blocking collectives  16.4 us (28%)
  starting transfers between devices  14.4 us (25%)
  Pallas kernels  10.1 us (17%)
    all_to_all x1, blocking collectives, per_device(): lax.all_to_all(active, ('expert', 'dp'), split_axis=0, concat_axis=0, til...  16.4 us
    pallas_call x5, Pallas kernels, local_call(): pl.pallas_call(kernel, out_shape=outs, in_specs=[HBM if i in hbm else VME...  10.1 us
    ppermute x6, starting transfers between devices, swap(): return lax.ppermute(x, axis, [(i, i ^ mask) for i in range(size)])  7.63 us
    all_to_all x1, waiting for transfers between devices, per_device(): lax.all_to_all(partial_sums, 'expert', split_axis=0, concat_axis=0, tiled...  6.48 us
    all_to_all x1, waiting for transfers between devices, per_device(): lax.all_to_all(tokens, 'expert', split_axis=0, concat_axis=0, tiled=True,...  6.34 us
    ppermute x6, waiting for transfers between devices, swap(): return lax.ppermute(x, axis, [(i, i ^ mask) for i in range(size)])  3.73 us
    all_to_all x1, starting transfers between devices, per_device(): lax.all_to_all(partial_sums, 'expert', split_axis=0, concat_axis=0, tiled...  3.4 us
    all_to_all x1, starting transfers between devices, per_device(): lax.all_to_all(tokens, 'expert', split_axis=0, concat_axis=0, tiled=True,...  3.38 us
  transfers between devices with their start and end apart: 8, of which 4 were waited for; matrix products, arithmetic and copies ran while one was open for 0% of the time, Pallas kernels for 9%

profile of v6, /device:TPU:0, one launch (start us, length us, event | category | flops | bytes accessed | tf_op | source)
XLA Modules:
  0.0 57.7 jit_solution(3358377819272113333)
XLA Ops:
  0.0 4.0 %collective-permute-start.2 = (bf16[4,2,3584]{2,1,0:T(2,128)(2,1)}, bf16[4,2,3584]{2,1,0:T(2,128)(2,1)S(1)}, u32[]{:S(2)}, u32[]{:S(2)}) collective-permute-start(bf16[4,2,3584]{2,1,0:T(2,128)(2,1)} %param.21), channel_id=1, source_target_pairs={{0,8},{2,10},{4,12},{6,14},{8,0},{10,2},{12,4},{14,6},{1,9},{3,11}... | collective-permute-start | bytes 172040 | tf_op jit(solution)/shard_map/ppermute | solution.py:208
  4.0 4.6 %attention.1 = bf16[4,8,3584]{2,1,0:T(8,128)(2,1)} custom-call(s32[8,32]{1,0:T(8,128)} %bitcast.17, s32[1,32]{1,0:T(1,128)} %bitcast.18, s32[1,32]{1,0:T(1,128)} %bitcast.19, bf16[32,576]{1,0:T(8,128)(2,1)} %bitcast.16, bf16[512,128]{1,0:T(8,128)(2,1)} %bitcast.15, bf16[128,3584]{1,0:T(8,128)(2,1)} %bitcast.14, bf16[2048,576]{1,0:T(8,128)(2,1)} %bitcast.13), custom_call_target="tpu_custom_call" | custom-call | flops 4000000000 | bytes 1 | tf_op jit(solution)/shard_map/attention/pallas_call | solution.py:212
  8.6 3.4 %all-to-all-start = ((bf16[4,8,3584]{2,1,0:T(8,128)(2,1)}), bf16[4,8,3584]{2,1,0:T(8,128)(2,1)S(1)}, u32[]{:S(2)}, u32[]{:S(2)}) async-start(bf16[4,8,3584]{2,1,0:T(8,128)(2,1)} %attention.1), calls=%async_computation | async-start | bytes 458752 | tf_op jit(solution)/shard_map/all_to_all | solution.py:264
  12.1 0.0 collective-permute-done.2
  12.2 1.6 %collective-permute-start.3 = (bf16[16,3584]{1,0:T(8,128)(2,1)S(1)}, bf16[16,3584]{1,0:T(8,128)(2,1)S(1)}, u32[]{:S(2)}, u32[]{:S(2)}) collective-permute-start(bf16[16,3584]{1,0:T(8,128)(2,1)S(1)} %constant_dynamic-update-slice_fusion), channel_id=1, source_target_pairs={{0,2},{2,0},{4,6},{6,4},{8,10},{10,8},{12,14},{14,12},{1,3},{3,1},... | collective-permute-start | bytes 344072 | tf_op jit(solution)/shard_map/ppermute | solution.py:208
  13.7 6.5 %all-to-all-done.parts_ref = bf16[4,8,3584]{2,1,0:T(8,128)(2,1)S(1)} async-done(((bf16[4,8,3584]{2,1,0:T(8,128)(2,1)}), bf16[4,8,3584]{2,1,0:T(8,128)(2,1)S(1)}, u32[]{:S(2)}, u32[]{:S(2)}) %all-to-all-start) | async-done | bytes 229408 | tf_op jit(solution)/shard_map/all_to_all | solution.py:264
  20.2 0.0 copy-done
  20.2 0.1 far_sum.1.mine_ref
  20.3 1.6 %collective-permute-start = (bf16[8,3584]{1,0:T(8,128)(2,1)S(1)}, bf16[8,3584]{1,0:T(8,128)(2,1)S(1)}, u32[]{:S(2)}, u32[]{:S(2)}) collective-permute-start(bf16[8,3584]{1,0:T(8,128)(2,1)S(1)} %far_sum.1.mine_ref), channel_id=1, source_target_pairs={{0,2},{2,0},{4,6},{6,4},{8,10},{10,8},{12,14},{14,12},{1,3},{3,1},... | collective-permute-start | bytes 172040 | tf_op jit(solution)/shard_map/ppermute | solution.py:208
  21.8 0.0 collective-permute-done.3
  21.9 0.4 collective-permute-start.4
  22.3 2.2 %collective-permute-done.theirs_ref = bf16[8,3584]{1,0:T(8,128)(2,1)S(1)} collective-permute-done((bf16[8,3584]{1,0:T(8,128)(2,1)S(1)}, bf16[8,3584]{1,0:T(8,128)(2,1)S(1)}, u32[]{:S(2)}, u32[]{:S(2)}) %collective-permute-start) | collective-permute-done | bytes 57376 | tf_op jit(solution)/shard_map/ppermute | solution.py:208
  24.5 0.8 %norm_draft.1 = bf16[4,8,3584]{2,1,0:T(8,128)(2,1)} custom-call(bf16[8,3584]{1,0:T(8,128)(2,1)S(1)} %far_sum.1.mine_ref, bf16[8,3584]{1,0:T(8,128)(2,1)S(1)} %collective-permute-done.theirs_ref, bf16[1,3584]{1,0:T(2,128)(2,1)S(1)} %reshape.26.gain_ref), custom_call_target="tpu_custom_call" | custom-call | flops 1000000000 | bytes 1 | tf_op jit(solution)/shard_map/norm_draft/pallas_call | solution.py:212
  25.3 3.4 %all-to-all-start.1 = ((bf16[4,8,3584]{2,1,0:T(8,128)(2,1)}), bf16[4,8,3584]{2,1,0:T(8,128)(2,1)S(1)}, u32[]{:S(2)}, u32[]{:S(2)}) async-start(bf16[4,8,3584]{2,1,0:T(8,128)(2,1)} %norm_draft.1), calls=%async_computation.1 | async-start | bytes 458752 | tf_op jit(solution)/shard_map/all_to_all | solution.py:279
  28.8 0.0 collective-permute-done.4
  28.8 0.1 collective-permute-start.5
  28.9 6.3 %all-to-all-done.1.draft_ref = bf16[4,8,3584]{2,1,0:T(8,128)(2,1)S(1)} async-done(((bf16[4,8,3584]{2,1,0:T(8,128)(2,1)}), bf16[4,8,3584]{2,1,0:T(8,128)(2,1)S(1)}, u32[]{:S(2)}, u32[]{:S(2)}) %all-to-all-start.1) | async-done | bytes 229408 | tf_op jit(solution)/shard_map/all_to_all | solution.py:279
  35.2 0.0 collective-permute-start.1
  35.2 1.5 %collective-permute-done.1.draft_other_ref = bf16[4,8,3584]{2,1,0:T(8,128)(2,1)S(1)} collective-permute-done((bf16[4,8,3584]{2,1,0:T(8,128)(2,1)S(1)}, bf16[4,8,3584]{2,1,0:T(8,128)(2,1)S(1)}, u32[]{:S(2)}, u32[]{:S(2)}) %collective-permute-start.1) | collective-permute-done | bytes 229408 | tf_op jit(solution)/shard_map/ppermute | solution.py:208
  36.7 0.0 collective-permute-done.5.verify_other_ref
  36.7 3.7 %expert.1 = bf16[16,3,4,1024]{3,2,1,0:T(4,128)(2,1)S(1)} custom-call(bf16[4,8,3584]{2,1,0:T(8,128)(2,1)S(1)} %all-to-all-done.1.draft_ref, bf16[4,8,3584]{2,1,0:T(8,128)(2,1)S(1)} %collective-permute-done.1.draft_other_ref, bf16[64,3584]{1,0:T(8,128)(2,1)S(1)} %constant_dynamic-update-slice_fusion.4.verify_ref, ...), custom_call_target="tpu_custom_call" | custom-call | flops 4000000000 | bytes 1 | tf_op jit(solution)/shard_map/expert/pallas_call | solution.py:212
  40.4 16.4 %all_to_all.15.back_ref = bf16[16,3,4,1024]{3,2,1,0:T(4,128)(2,1)S(1)} all-to-all(bf16[16,3,4,1024]{3,2,1,0:T(4,128)(2,1)S(1)} %expert.1), channel_id=1, replica_groups=mesh['groups'=2,'expert'=8,'dp'=2] {'expert','dp'}, dimensions={0} | all-to-all | bytes 786432 | tf_op jit(solution)/shard_map/all_to_all | solution.py:315
  56.7 0.0 copy-done.1
  56.8 0.9 %select.1 = bf16[4,3,8,1024]{3,2,1,0:T(8,128)(2,1)} custom-call(s32[3,4,8]{2,1,0:T(4,128)S(1)} %bitcast.10, f32[3,4,8]{2,1,0:T(4,128)S(1)} %bitcast.11, bf16[16,3,4,1024]{3,2,1,0:T(4,128)(2,1)S(1)} %all_to_all.15.back_ref), custom_call_target="tpu_custom_call" | custom-call | flops 1000000000 | bytes 1 | tf_op jit(solution)/shard_map/select/pallas_call | solution.py:212
  (17 shorter events, 0.1 us)
Async XLA Ops:
  0.0 12.1 %collective-permute-start.2 = (bf16[4,2,3584]{2,1,0:T(2,128)(2,1)}, bf16[4,2,3584]{2,1,0:T(2,128)(2,1)S(1)}, u32[]{:S(2)}, u32[]{:S(2)}) collective-permute-start(bf16[4,2,3584]{2,1,0:T(2,128)(2,1)} %param.21), channel_id=1, source_target_pairs={{0,8},{2,10},{4,12},{6,14},{8,0},{10,2},{12,4},{14,6},{1,9},{3,11}... | collective-permute-start | bytes 172040 | tf_op jit(solution)/shard_map/ppermute | solution.py:208
  4.0 8.0 %copy-start.3 = (bf16[4,2,3584]{2,1,0:T(2,128)(2,1)S(1)}, bf16[4,2,3584]{2,1,0:T(2,128)(2,1)}, u32[]{:S(2)}) copy-start(bf16[4,2,3584]{2,1,0:T(2,128)(2,1)} %param.21) | copy-start | bytes 172036
  4.0 8.1 %copy-start.4 = (bf16[3584]{0:T(1024)(128)(2,1)S(1)}, bf16[3584]{0:T(1024)(128)(2,1)}, u32[]{:S(2)}) copy-start(bf16[3584]{0:T(1024)(128)(2,1)} %param.22) | copy-start | bytes 21508
  4.0 16.2 %copy-start = (bf16[4,3584]{1,0:T(4,128)(2,1)S(1)}, bf16[4,3584]{1,0:T(4,128)(2,1)}, u32[]{:S(2)}) copy-start(bf16[4,3584]{1,0:T(4,128)(2,1)} %residual_ref.1) | copy-start | bytes 86020
  8.6 11.6 %all-to-all-start = ((bf16[4,8,3584]{2,1,0:T(8,128)(2,1)}), bf16[4,8,3584]{2,1,0:T(8,128)(2,1)S(1)}, u32[]{:S(2)}, u32[]{:S(2)}) async-start(bf16[4,8,3584]{2,1,0:T(8,128)(2,1)} %attention.1), calls=%async_computation | async-start | bytes 458752 | tf_op jit(solution)/shard_map/all_to_all | solution.py:264
  12.2 9.7 %collective-permute-start.3 = (bf16[16,3584]{1,0:T(8,128)(2,1)S(1)}, bf16[16,3584]{1,0:T(8,128)(2,1)S(1)}, u32[]{:S(2)}, u32[]{:S(2)}) collective-permute-start(bf16[16,3584]{1,0:T(8,128)(2,1)S(1)} %constant_dynamic-update-slice_fusion), channel_id=1, source_target_pairs={{0,2},{2,0},{4,6},{6,4},{8,10},{10,8},{12,14},{14,12},{1,3},{3,1},... | collective-permute-start | bytes 344072 | tf_op jit(solution)/shard_map/ppermute | solution.py:208
  20.3 4.2 %collective-permute-start = (bf16[8,3584]{1,0:T(8,128)(2,1)S(1)}, bf16[8,3584]{1,0:T(8,128)(2,1)S(1)}, u32[]{:S(2)}, u32[]{:S(2)}) collective-permute-start(bf16[8,3584]{1,0:T(8,128)(2,1)S(1)} %far_sum.1.mine_ref), channel_id=1, source_target_pairs={{0,2},{2,0},{4,6},{6,4},{8,10},{10,8},{12,14},{14,12},{1,3},{3,1},... | collective-permute-start | bytes 172040 | tf_op jit(solution)/shard_map/ppermute | solution.py:208
  21.9 6.9 %collective-permute-start.4 = (bf16[32,3584]{1,0:T(8,128)(2,1)S(1)}, bf16[32,3584]{1,0:T(8,128)(2,1)S(1)}, u32[]{:S(2)}, u32[]{:S(2)}) collective-permute-start(bf16[32,3584]{1,0:T(8,128)(2,1)S(1)} %constant_dynamic-update-slice_fusion.2), channel_id=1, source_target_pairs={{0,4},{2,6},{4,0},{6,2},{8,12},{10,14},{12,8},{14,10},{1,5},{3,7},... | collective-permute-start | bytes 688136 | tf_op jit(solution)/shard_map/ppermute | solution.py:208
  25.3 9.9 %all-to-all-start.1 = ((bf16[4,8,3584]{2,1,0:T(8,128)(2,1)}), bf16[4,8,3584]{2,1,0:T(8,128)(2,1)S(1)}, u32[]{:S(2)}, u32[]{:S(2)}) async-start(bf16[4,8,3584]{2,1,0:T(8,128)(2,1)} %norm_draft.1), calls=%async_computation.1 | async-start | bytes 458752 | tf_op jit(solution)/shard_map/all_to_all | solution.py:279
  28.8 7.9 %collective-permute-start.5 = (bf16[64,3584]{1,0:T(8,128)(2,1)S(1)}, bf16[64,3584]{1,0:T(8,128)(2,1)S(1)}, u32[]{:S(2)}, u32[]{:S(2)}) collective-permute-start(bf16[64,3584]{1,0:T(8,128)(2,1)S(1)} %constant_dynamic-update-slice_fusion.4.verify_ref), channel_id=1, source_target_pairs={{0,1},{1,0},{2,3},{3,2},{4,5},{5,4},{6,7},{7,6},{8,9},{9,8},{10,11... | collective-permute-start | bytes 1376264 | tf_op jit(solution)/shard_map/ppermute | solution.py:208
  35.2 1.5 %collective-permute-start.1 = (bf16[4,8,3584]{2,1,0:T(8,128)(2,1)S(1)}, bf16[4,8,3584]{2,1,0:T(8,128)(2,1)S(1)}, u32[]{:S(2)}, u32[]{:S(2)}) collective-permute-start(bf16[4,8,3584]{2,1,0:T(8,128)(2,1)S(1)} %all-to-all-done.1.draft_ref), channel_id=1, source_target_pairs={{0,1},{1,0},{2,3},{3,2},{4,5},{5,4},{6,7},{7,6},{8,9},{9,8},{10,11... | collective-permute-start | bytes 688136 | tf_op jit(solution)/shard_map/ppermute | solution.py:208
  36.7 20.1 %copy-start.1 = (s32[4,3,8]{2,0,1:T(4,128)S(1)}, s32[4,3,8]{2,0,1:T(4,128)}, u32[]{:S(2)}) copy-start(s32[4,3,8]{2,0,1:T(4,128)} %param.23) | copy-start | bytes 1156
  36.7 20.1 %copy-start.2 = (f32[4,3,8]{2,0,1:T(4,128)S(1)}, f32[4,3,8]{2,0,1:T(4,128)}, u32[]{:S(2)}) copy-start(f32[4,3,8]{2,0,1:T(4,128)} %param.24) | copy-start | bytes 1156
